TPU v7x, 512 devices: a whole 4x4x16 slice. The times are simulated.
512 devices in a mesh: section: 8 (over x, core), expert: 64 (over z, y).
Axes of the slice: x: 4, y: 4, z: 16, core: 2. Of those that a mesh axis runs over, the one named last changes fastest.
Arguments:
- fwd_sent: bfloat16 [8, 4096, 3584], P('section', 'expert'), may hold values from -6 to 6
- grad_sent: bfloat16 [8, 4096, 3584], P('section', 'expert'), may hold values from -6 to 6
- saved_scale: float32 [8, 4096], P('section', 'expert'), may hold values from 0.5 to 2
- norm_gain: float32 [8, 3584], P('section'), may hold values from 0.1 to 1.9
- w_in: bfloat16 [8, 64, 3584, 256], P('section', 'expert'), may hold values from -0.09375 to 0.09375
- w_down: bfloat16 [8, 64, 128, 3584], P('section', 'expert'), may hold values from -0.1875 to 0.1875
- saved_pre: bfloat16 [8, 64, 512, 256], P('section', 'expert'), may hold values from -5 to 5
- route_fwd: int32 [8, 4096, 1], P('section', 'expert'), may hold values from 0 to 7; in each aligned block of 64 rows (0 to 63, 64 to 127, ..., all dimensions but the last counted through in order) at most 8 rows name the same one
- route_bwd: int32 [8, 4096, 1], P('section', 'expert'), may hold values from 0 to 7; in each aligned block of 64 rows (0 to 63, 64 to 127, ..., all dimensions but the last counted through in order) at most 8 rows name the same one
- weight_fwd: float32 [8, 4096], P('section', 'expert'), may hold values from 0.2 to 1
- weight_bwd: float32 [8, 4096], P('section', 'expert'), may hold values from 0.2 to 1
Outputs:
- forward_out: bfloat16 [8, 4096, 3584], P('section', 'expert')
- backward_out: bfloat16 [8, 4096, 3584], P('section', 'expert')
Inputs may be any that keep to these rules, and one draw needn't show every extreme that they name: `route_fwd`: in every layer, the 64 tokens of one aligned block route to each expert exactly 8 times. `route_bwd`: in every layer, the 64 tokens of one aligned block route to each expert exactly 8 times.
All inputs are finite; a program needn't handle non-finite values.
Results may differ from a plain program's by a relative error of at most 0.005.
Values may be sent and summed in bfloat16 or wider, within the bound.
No kernel may reach another device: no remote copies, remote signals or barrier semaphores. Data moves between devices by JAX's collectives and lax.ppermute only.
A program may use at most 64 MiB of HBM per device.

v0:
```python
import jax
import jax.numpy as jnp
from jax import lax
from jax.sharding import PartitionSpec as P

EXPERTS = 8
CAP = 8


EPSILON = 1e-06


def from_behind(block, axis, distance):
    devices = range(lax.axis_size(axis))
    route = [((i - distance) % len(devices), i) for i in devices]
    return lax.ppermute(block, axis, route)


def slot_positions(choices):
    expert_ids = jnp.arange(EXPERTS, dtype=jnp.int32)
    onehot = (choices[:, None] == expert_ids[None, :]).astype(jnp.int32)
    earlier = jnp.cumsum(onehot, axis=0) - onehot
    slot_rank = jnp.sum(earlier * onehot, axis=1)
    return choices * CAP + slot_rank


def slot_table(positions):
    columns = jnp.arange(EXPERTS * CAP, dtype=jnp.int32)
    return (positions[:, None] == columns[None, :]).astype(jnp.bfloat16)


def normalize(values, gain_row):
    inverse = lax.rsqrt(jnp.mean(values * values, axis=-1, keepdims=True) + EPSILON)
    return (values * inverse * gain_row, inverse)


def pack_rows(tokens, choices, copies):
    positions = slot_positions(choices)
    slot_onehot = slot_table(positions)
    packed = lax.dot_general(
        slot_onehot, tokens, (((0,), (0,)), ((), ())), preferred_element_type=jnp.float32
    ).astype(jnp.bfloat16)
    feature_count = tokens.shape[1]
    spread = jnp.broadcast_to(
        packed.reshape(EXPERTS, 1, CAP, feature_count), (EXPERTS, copies, CAP, feature_count)
    )
    return (spread.reshape(EXPERTS * copies, CAP, feature_count), positions)


def unpack_rows(returned, positions, copies):
    feature_count = returned.shape[2]
    summed = jnp.sum(
        returned.reshape(EXPERTS, copies, CAP, feature_count).astype(jnp.float32), axis=1
    )
    return jnp.take(summed.reshape(EXPERTS * CAP, feature_count), positions, axis=0)


def forward_slice(row_block, weights_in, weights_down):
    pre_act = jnp.dot(row_block, weights_in, preferred_element_type=jnp.float32)
    half_width = weights_in.shape[1] // 2
    hidden_act = (jax.nn.silu(pre_act[:, :half_width]) * pre_act[:, half_width:]).astype(
        jnp.bfloat16
    )
    return jnp.dot(hidden_act, weights_down, preferred_element_type=jnp.float32).astype(
        jnp.bfloat16
    )


def backward_slice(row_block, weights_in, weights_down, saved):
    contract_dims = (((1,), (1,)), ((), ()))
    grad_act = lax.dot_general(
        row_block, weights_down, contract_dims, preferred_element_type=jnp.float32
    )
    half_width = saved.shape[1] // 2
    pre_act = saved.astype(jnp.float32)
    gate_pre = pre_act[:, :half_width]
    up_pre = pre_act[:, half_width:]
    sigmoid_gate = jax.nn.sigmoid(gate_pre)
    grad_gate = grad_act * up_pre * sigmoid_gate * (1.0 + gate_pre * (1.0 - sigmoid_gate))
    grad_up = grad_act * gate_pre * sigmoid_gate
    grad_pre = jnp.concatenate([grad_gate, grad_up], axis=1).astype(jnp.bfloat16)
    return lax.dot_general(
        grad_pre, weights_in, contract_dims, preferred_element_type=jnp.float32
    ).astype(jnp.bfloat16)


def shards(
    fwd_sent,
    grad_sent,
    saved_scale,
    norm_gain,
    w_in,
    w_down,
    saved_pre,
    route_fwd,
    route_bwd,
    weight_fwd,
    weight_bwd,
):
    peers = lax.axis_size("expert")
    copies = peers // EXPERTS
    arrive = from_behind(fwd_sent[0], "section", 1)
    grad_back = from_behind(grad_sent[0], "section", -1)
    gain_row = norm_gain[0]
    arrive_wide = arrive.astype(jnp.float32)
    normed, _ = normalize(arrive_wide, gain_row)
    back_wide = grad_back.astype(jnp.float32)
    scaled = (back_wide * weight_bwd[0][:, None]).astype(jnp.bfloat16)
    weights_in = w_in[0, 0]
    weights_down = w_down[0, 0]
    saved = saved_pre[0, 0]
    send_forward, positions_fwd = pack_rows(normed.astype(jnp.bfloat16), route_fwd[0, :, 0], copies)
    send_backward, positions_bwd = pack_rows(scaled, route_bwd[0, :, 0], copies)
    arrived_forward = lax.all_to_all(
        send_forward, "expert", split_axis=0, concat_axis=0, tiled=True
    )
    flat_rows = arrived_forward.reshape(-1, arrived_forward.shape[2])
    returned_forward = lax.all_to_all(
        forward_slice(flat_rows, weights_in, weights_down).reshape(arrived_forward.shape),
        "expert",
        split_axis=0,
        concat_axis=0,
        tiled=True,
    )
    arrived_backward = lax.all_to_all(
        send_backward, "expert", split_axis=0, concat_axis=0, tiled=True
    )
    flat_rows = arrived_backward.reshape(-1, arrived_backward.shape[2])
    returned_backward = lax.all_to_all(
        backward_slice(flat_rows, weights_in, weights_down, saved).reshape(arrived_backward.shape),
        "expert",
        split_axis=0,
        concat_axis=0,
        tiled=True,
    )
    mixture = unpack_rows(returned_forward, positions_fwd, copies)
    grad_norm = unpack_rows(returned_backward, positions_bwd, copies)
    forward_out = (arrive_wide + weight_fwd[0][:, None] * mixture).astype(jnp.bfloat16)
    grad_start = saved_scale[0][:, None] * gain_row * grad_norm
    backward_out = (back_wide + grad_start).astype(jnp.bfloat16)
    return (forward_out[None], backward_out[None])


def solution(mesh):
    in_specs = (
        P("section", "expert", None),
        P("section", "expert", None),
        P("section", "expert"),
        P("section", None),
        P("section", "expert", None, None),
        P("section", "expert", None, None),
        P("section", "expert", None, None),
        P("section", "expert", None),
        P("section", "expert", None),
        P("section", "expert"),
        P("section", "expert"),
    )
    out_specs = (P("section", "expert", None), P("section", "expert", None))
    return jax.shard_map(shards, mesh=mesh, in_specs=in_specs, out_specs=out_specs, check_vma=False)
```

profile of v0, /device:TPU:6, one launch (start us, length us, event | category | flops | bytes accessed | tf_op | source)
XLA Modules:
  0.0 729.4 jit_solution(9609713985892341965)
XLA Ops:
  3.4 3.8 collective-permute-done.1
  7.2 1.0 fusion.3
  8.3 2.1 broadcast_in_dim.40
  10.4 19.1 %all-to-all-start.2 = ((bf16[64,8,3584]{2,1,0:T(8,128)(2,1)}), bf16[64,8,3584]{2,1,0:T(8,128)(2,1)}, u32[]{:S(2)}, u32[]{:S(2)}) async-start(bf16[64,8,3584]{2,1,0:T(8,128)(2,1)} %bitcast.58), calls=%async_computation.2 | async-start | bytes 7340032 | tf_op jit(solution)/shard_map/all_to_all | solution.py:125
  29.5 2.3 collective-permute-start
  32.2 5.2 collective-permute-done
  38.0 154.0 %all-to-all-done.2 = bf16[64,8,3584]{2,1,0:T(8,128)(2,1)} async-done(((bf16[64,8,3584]{2,1,0:T(8,128)(2,1)}), bf16[64,8,3584]{2,1,0:T(8,128)(2,1)}, u32[]{:S(2)}, u32[]{:S(2)}) %all-to-all-start.2) | async-done | bytes 3670048 | tf_op jit(solution)/shard_map/all_to_all | solution.py:125
  192.0 2.2 broadcast_in_dim.37
  194.2 11.7 %all-to-all-start = ((bf16[64,8,3584]{2,1,0:T(8,128)(2,1)}), bf16[64,8,3584]{2,1,0:T(8,128)(2,1)}, u32[]{:S(2)}, u32[]{:S(2)}) async-start(bf16[64,8,3584]{2,1,0:T(8,128)(2,1)} %bitcast.59), calls=%async_computation | async-start | bytes 7340032 | tf_op jit(solution)/shard_map/all_to_all | solution.py:114
  206.0 3.1 fusion.27
  209.2 3.1 fusion.1
  212.2 162.1 %all-to-all-done = bf16[64,8,3584]{2,1,0:T(8,128)(2,1)} async-done(((bf16[64,8,3584]{2,1,0:T(8,128)(2,1)}), bf16[64,8,3584]{2,1,0:T(8,128)(2,1)}, u32[]{:S(2)}, u32[]{:S(2)}) %all-to-all-start) | async-done | bytes 3670048 | tf_op jit(solution)/shard_map/all_to_all | solution.py:114
  374.3 6.1 all-to-all-start.3
  380.4 3.1 fusion.6
  383.5 2.9 fusion
  386.4 161.0 %all-to-all-done.3 = bf16[64,8,3584]{2,1,0:T(8,128)(2,1)} async-done(((bf16[64,8,3584]{2,1,0:T(8,128)(2,1)}), bf16[64,8,3584]{2,1,0:T(8,128)(2,1)}, u32[]{:S(2)}, u32[]{:S(2)}) %all-to-all-start.3) | async-done | bytes 3670048 | tf_op jit(solution)/shard_map/all_to_all | solution.py:129
  547.4 6.1 all-to-all-start.1
  553.6 2.6 convert_reduce_fusion
  556.2 1.8 gather_fusion.1
  558.0 162.5 %all-to-all-done.1 = bf16[64,8,3584]{2,1,0:T(8,128)(2,1)} async-done(((bf16[64,8,3584]{2,1,0:T(8,128)(2,1)}), bf16[64,8,3584]{2,1,0:T(8,128)(2,1)}, u32[]{:S(2)}, u32[]{:S(2)}) %all-to-all-start.1) | async-done | bytes 3670048 | tf_op jit(solution)/shard_map/all_to_all | solution.py:118
  720.5 2.6 convert_reduce_fusion.1
  723.2 1.8 gather_fusion
  725.0 2.3 fusion.20
  727.3 2.2 fusion.18
  (36 shorter events, 3.9 us)
Async XLA Ops:
  0.6 208.5 %copy-start = (bf16[1,1,3584,256]{3,2,1,0:T(8,128)(2,1)S(1)}, bf16[1,1,3584,256]{3,2,1,0:T(8,128)(2,1)}, u32[]{:S(2)}) copy-start(bf16[1,1,3584,256]{3,2,1,0:T(8,128)(2,1)} %param.17) | copy-start | bytes 5505028
  0.6 6.6 collective-permute-start.1
  7.2 3.1 copy-start.1
  10.3 19.1 %copy-start.8 = (bf16[1,64,3584]{2,1,0:T(8,128)(2,1)S(1)}, bf16[1,64,3584]{2,1,0:T(8,128)(2,1)}, u32[]{:S(2)}) copy-start(bf16[1,64,3584]{2,1,0:T(8,128)(2,1)} %param.13) | copy-start | bytes 1376260
  10.3 21.4 %copy-start.5 = (s32[1,64,1]{1,2,0:T(1,128)S(1)}, s32[1,64,1]{1,2,0:T(1,128)}, u32[]{:S(2)}) copy-start(s32[1,64,1]{1,2,0:T(1,128)} %param.20) | copy-start | bytes 772
  10.4 21.6 %copy-start.4 = (f32[1,3584]{1,0:T(1,128)S(1)}, f32[1,3584]{1,0:T(1,128)}, u32[]{:S(2)}) copy-start(f32[1,3584]{1,0:T(1,128)} %param.16) | copy-start | bytes 43012
  10.4 181.7 %all-to-all-start.2 = ((bf16[64,8,3584]{2,1,0:T(8,128)(2,1)}), bf16[64,8,3584]{2,1,0:T(8,128)(2,1)}, u32[]{:S(2)}, u32[]{:S(2)}) async-start(bf16[64,8,3584]{2,1,0:T(8,128)(2,1)} %bitcast.58), calls=%async_computation.2 | async-start | bytes 7340032 | tf_op jit(solution)/shard_map/all_to_all | solution.py:125
  29.5 7.9 %collective-permute-start = (bf16[64,3584]{1,0:T(8,128)(2,1)S(1)}, bf16[64,3584]{1,0:T(8,128)(2,1)S(1)}, u32[]{:S(2)}, u32[]{:S(2)}) collective-permute-start(bf16[64,3584]{1,0:T(8,128)(2,1)S(1)} %bitcast.68), channel_id=1, source_target_pairs={{448,0},{0,64},{64,128},{128,192},{192,256},{256,320},{320,384},{3... | collective-permute-start | bytes 1376264 | tf_op jit(solution)/shard_map/ppermute | solution.py:16
  194.2 11.8 %copy-start.3 = (bf16[1,1,512,256]{3,2,1,0:T(8,128)(2,1)S(1)}, bf16[1,1,512,256]{3,2,1,0:T(8,128)(2,1)}, u32[]{:S(2)}) copy-start(bf16[1,1,512,256]{3,2,1,0:T(8,128)(2,1)} %param.19) | copy-start | bytes 786436
  194.2 11.8 %copy-start.2 = (bf16[1,1,128,3584]{3,2,1,0:T(8,128)(2,1)S(1)}, bf16[1,1,128,3584]{3,2,1,0:T(8,128)(2,1)}, u32[]{:S(2)}) copy-start(bf16[1,1,128,3584]{3,2,1,0:T(8,128)(2,1)} %param.18) | copy-start | bytes 2752516
  194.2 180.1 %all-to-all-start = ((bf16[64,8,3584]{2,1,0:T(8,128)(2,1)}), bf16[64,8,3584]{2,1,0:T(8,128)(2,1)}, u32[]{:S(2)}, u32[]{:S(2)}) async-start(bf16[64,8,3584]{2,1,0:T(8,128)(2,1)} %bitcast.59), calls=%async_computation | async-start | bytes 7340032 | tf_op jit(solution)/shard_map/all_to_all | solution.py:114
  374.3 173.1 %all-to-all-start.3 = ((bf16[64,8,3584]{2,1,0:T(8,128)(2,1)}), bf16[64,8,3584]{2,1,0:T(8,128)(2,1)}, u32[]{:S(2)}, u32[]{:S(2)}) async-start(bf16[64,8,3584]{2,1,0:T(8,128)(2,1)} %fusion.1), calls=%async_computation.3 | async-start | bytes 7340032 | tf_op jit(solution)/shard_map/all_to_all | solution.py:129
  547.4 173.1 %all-to-all-start.1 = ((bf16[64,8,3584]{2,1,0:T(8,128)(2,1)}), bf16[64,8,3584]{2,1,0:T(8,128)(2,1)}, u32[]{:S(2)}, u32[]{:S(2)}) async-start(bf16[64,8,3584]{2,1,0:T(8,128)(2,1)} %fusion), calls=%async_computation.1 | async-start | bytes 7340032 | tf_op jit(solution)/shard_map/all_to_all | solution.py:118
  723.1 1.8 copy-start.6
  723.2 4.1 copy-start.7
where the time goes:
time: 730 us; the launch traced here: 729 us
  waiting for transfers between devices  649 us (89%)
  starting transfers between devices  45.6 us (6%)
  matrix products  13.7 us (2%)
  other arithmetic  12.8 us (2%)
  local copies, waits for them, and re-layouts  7.83 us (1%)
    all_to_all x1, waiting for transfers between devices, shards(): lax.all_to_all(forward_slice(flat_rows, weights_in, weights_down).reshape...  163 us
    all_to_all x1, waiting for transfers between devices, shards(): lax.all_to_all(send_forward, 'expert', split_axis=0, concat_axis=0, tiled...  162 us
    all_to_all x1, waiting for transfers between devices, shards(): lax.all_to_all(backward_slice(flat_rows, weights_in, weights_down, saved)...  161 us
    all_to_all x1, waiting for transfers between devices, shards(): lax.all_to_all(send_backward, 'expert', split_axis=0, concat_axis=0, tile...  154 us
    all_to_all x1, starting transfers between devices, shards(): lax.all_to_all(send_backward, 'expert', split_axis=0, concat_axis=0, tile...  19.1 us
  transfers between devices with their start and end apart: 6, of which 6 were waited for; matrix products, arithmetic and copies ran while one was open for 3% of the time, Pallas kernels for 0%

commit v1 on v0

v1 whole, which is shorter than its diff:
```python
import jax
import jax.numpy as jnp
from jax import lax
from jax.experimental import pallas as pl
from jax.experimental.pallas import tpu as pltpu
from jax.sharding import PartitionSpec as P

EXPERTS = 8
CAP = 8
ROWS = 4
BLOCK = EXPERTS * CAP
EPSILON = 1e-06

FIRST = 2688
LAST = 896
DOWN = FIRST + LAST
NEXT = 2 * FIRST
TOTAL = NEXT + 256
WIDTH = 256
HIDDEN = 128
VMEM_LIMIT = 40 * 1024 * 1024


def shift_section(block, distance):
    size = lax.axis_size("section")
    return lax.ppermute(block, "section", [((i - distance) % size, i) for i in range(size)])


def shift_y(block, distance):
    size = lax.axis_size("expert")
    route = [(k, k - k % ROWS + (k + distance) % ROWS) for k in range(size)]
    return lax.ppermute(block, "expert", route)


def swap_z(block):
    size = lax.axis_size("expert")
    return lax.ppermute(block, "expert", [(k, k ^ ROWS) for k in range(size)])


def exchange_z(block):
    groups = [[2 * ROWS * g + r for g in range(EXPERTS)] for r in range(2 * ROWS)]
    return lax.all_to_all(
        block, "expert", split_axis=0, concat_axis=0, axis_index_groups=groups, tiled=True
    )


def exchange_halves(block):
    return jnp.concatenate([exchange_z(block[:, :CAP]), exchange_z(block[:, CAP:])], axis=1)


def as_column(row):
    size = row.shape[1]
    down = lax.broadcasted_iota(jnp.int32, (size, size), 0)
    across = lax.broadcasted_iota(jnp.int32, (size, size), 1)
    spread = jnp.where(down == across, jnp.broadcast_to(row, (size, size)), 0.0)
    return jnp.sum(spread, axis=1, keepdims=True)


def pack_kernel(route_fwd, route_bwd, arrive, grad_back, gain, weight, send, table):
    chosen = jnp.concatenate(
        [as_column(route[...].astype(jnp.float32)) for route in (route_fwd, route_bwd)], axis=0
    )
    shape = (2 * BLOCK, 2 * BLOCK)
    token = lax.broadcasted_iota(jnp.int32, shape, 0)
    column = lax.broadcasted_iota(jnp.int32, shape, 1)
    same = (column >> 4).astype(jnp.float32) == chosen
    same &= ((column >> 3) & 1) == (token >> 6)
    before = (column < token).astype(jnp.bfloat16)
    rank = mm(before, same.astype(jnp.bfloat16))
    onehot = (same & (rank == (column & 7).astype(jnp.float32))).astype(jnp.bfloat16)
    table[...] = onehot
    wide = arrive[...].astype(jnp.float32)
    inverse = lax.rsqrt(jnp.mean(wide * wide, axis=-1, keepdims=True) + EPSILON)
    normed = (wide * inverse * gain[...]).astype(jnp.bfloat16)
    scaled = (grad_back[...].astype(jnp.float32) * as_column(weight[...])).astype(jnp.bfloat16)
    tokens = jnp.concatenate([normed, scaled], axis=0)
    send[...] = lax.dot_general(
        onehot, tokens, (((0,), (0,)), ((), ())), preferred_element_type=jnp.float32
    ).astype(send.dtype)


def finish_kernel(table, back, arrive, grad_back, weight, scale, gain, forward_out, backward_out):
    got = mm(table[...], back[...])
    wide = arrive[...].astype(jnp.float32)
    forward_out[...] = (wide + as_column(weight[...]) * got[:BLOCK]).astype(forward_out.dtype)
    back_wide = grad_back[...].astype(jnp.float32)
    grad_start = as_column(scale[...]) * gain[...] * got[BLOCK:]
    backward_out[...] = (back_wide + grad_start).astype(backward_out.dtype)


def gather_kernel(in_own, down_own, saved_next, saved_previous, held, sems):
    count = down_own.shape[1] // WIDTH
    pieces = [
        (in_own, held.at[pl.ds(0, DOWN)]),
        (saved_next, held.at[pl.ds(NEXT, 128)]),
        (saved_previous, held.at[pl.ds(NEXT + 128, 128)]),
    ]
    for c in range(count):
        pieces.append(
            (
                down_own.at[:, pl.ds(c * WIDTH, WIDTH)],
                held.at[pl.ds(DOWN + c * HIDDEN, HIDDEN)],
            )
        )
    copies = [pltpu.make_async_copy(p[0], p[1], sems.at[i]) for i, p in enumerate(pieces)]
    for copy in copies:
        copy.start()
    for copy in copies:
        copy.wait()


def fetch(sources, buffers, sems):
    copies = [pltpu.make_async_copy(s, b, sems.at[i]) for i, (s, b) in enumerate(zip(sources, buffers))]
    for copy in copies:
        copy.start()
    return copies


def mm(a, b):
    return jnp.dot(a, b, preferred_element_type=jnp.float32)


def mt(a, b):
    return lax.dot_general(a, b, (((1,), (1,)), ((), ())), preferred_element_type=jnp.float32)


def activate(pre):
    gate, up = pre[:, :HIDDEN], pre[:, HIDDEN:]
    return (gate / (1.0 + jnp.exp(-gate)) * up).astype(jnp.bfloat16)


def slope(grad_act, saved):
    wide = saved.astype(jnp.float32)
    gate, up = wide[:, :HIDDEN], wide[:, HIDDEN:]
    sigmoid = 1.0 / (1.0 + jnp.exp(-gate))
    grad_gate = grad_act * up * sigmoid * (1.0 + gate * (1.0 - sigmoid))
    grad_up = grad_act * gate * sigmoid
    return jnp.concatenate([grad_gate, grad_up], axis=1).astype(jnp.bfloat16)


def down_blocks(held, start, count):
    return [held[start + c * HIDDEN : start + (c + 1) * HIDDEN] for c in range(count)]


def across_blocks(rows, held, start):
    count = rows.shape[1] // WIDTH
    total = 0.0
    for c, block in enumerate(down_blocks(held, start, count)):
        total = total + mt(rows[:, c * WIDTH : (c + 1) * WIDTH], block)
    return total


def near_kernel(rows_fwd, rows_bwd, saved_own, *refs):
    sources, part, grad_part, buffers, sems = refs[:4], refs[4], refs[5], refs[6:10], refs[10]
    copies = fetch(sources, buffers, sems)
    own_in, own_down, behind, ahead = buffers
    count = rows_fwd.shape[1] // WIDTH
    copies[0].wait()
    copies[1].wait()
    acts = [activate(mm(rows_fwd[...], own_in[...]))]
    grads = [slope(mt(rows_bwd[...], own_down[...]), saved_own[...])]
    for i, near, saved in ((2, behind, NEXT), (3, ahead, NEXT + 128)):
        copies[i].wait()
        acts.append(activate(mm(rows_fwd[...], near[:DOWN])))
        grads.append(slope(across_blocks(rows_bwd, near, DOWN), near[saved : saved + 128]))
    for c in range(count):
        columns = slice(c * WIDTH, (c + 1) * WIDTH)
        block = slice(DOWN + c * HIDDEN, DOWN + (c + 1) * HIDDEN)
        total = mm(acts[0], own_down[:, columns])
        part[:, columns] = total + mm(acts[1], behind[block]) + mm(acts[2], ahead[block])
    for c in range(count * WIDTH // LAST):
        columns = slice(c * LAST, (c + 1) * LAST)
        total = mt(grads[0], own_in[columns])
        grad_part[:, columns] = total + mt(grads[1], behind[columns]) + mt(grads[2], ahead[columns])


def forward_kernel(rows, part, *refs):
    sources, out, buffers, sems = refs[:2], refs[2], refs[3:5], refs[5]
    copies = fetch(sources, buffers, sems)
    far_a, far_b = buffers
    copies[0].wait()
    pre = mm(rows[:, :FIRST], far_a[...])
    copies[1].wait()
    act = activate(pre + mm(rows[:, FIRST:], far_b[:LAST]))
    count = rows.shape[1] // WIDTH
    for c, block in enumerate(down_blocks(far_b, LAST, count)):
        columns = slice(c * WIDTH, (c + 1) * WIDTH)
        out[:, columns] = (part[:, columns] + mm(act, block)).astype(out.dtype)


def backward_kernel(rows, part, saved, *refs):
    sources, out, buffers, sems = refs[:2], refs[2], refs[3:5], refs[5]
    copies = fetch(sources, buffers, sems)
    far_a, far_b = buffers
    copies[0].wait()
    copies[1].wait()
    grad = slope(across_blocks(rows, far_b, LAST), saved[...])
    for c in range(rows.shape[1] // LAST):
        columns = slice(c * LAST, (c + 1) * LAST)
        weights = far_a[columns] if c * LAST < FIRST else far_b[:LAST]
        out[:, columns] = (part[:, columns] + mt(grad, weights)).astype(out.dtype)


def call(kernel, outs, whole, held=(), flops=0, traffic=8_000_000):
    in_vmem, left = pl.BlockSpec(memory_space=pltpu.VMEM), pl.BlockSpec(memory_space=pl.ANY)
    scratch = [pltpu.VMEM(h.shape, h.dtype) for h in held]
    scratch += [pltpu.SemaphoreType.DMA((len(held),))] if held else []
    return pl.pallas_call(
        kernel,
        out_shape=[jax.ShapeDtypeStruct(shape, dtype) for shape, dtype in outs],
        in_specs=[in_vmem] * len(whole) + [left] * len(held),
        out_specs=[in_vmem] * len(outs),
        scratch_shapes=scratch,
        compiler_params=pltpu.CompilerParams(vmem_limit_bytes=VMEM_LIMIT),
        cost_estimate=pl.CostEstimate(flops=flops, bytes_accessed=traffic, transcendentals=0),
    )(*whole, *held)


def shards(
    fwd_sent,
    grad_sent,
    saved_scale,
    norm_gain,
    w_in,
    w_down,
    saved_pre,
    route_fwd,
    route_bwd,
    weight_fwd,
    weight_bwd,
):
    features = fwd_sent.shape[2]
    place = lax.axis_index("expert")
    y = place % ROWS
    parity = (place // ROWS) % 2
    in_own, down_own = w_in[0, 0], w_down[0, 0]

    by_source = saved_pre[0, 0].reshape(EXPERTS, 2, ROWS, CAP, WIDTH)

    def saved_for(distance):
        column = lax.dynamic_index_in_dim(by_source, (y + distance) % ROWS, 2, keepdims=False)
        mine = lax.dynamic_index_in_dim(column, parity, 1, keepdims=False)
        other = lax.dynamic_index_in_dim(column, 1 - parity, 1, keepdims=False)
        return jnp.concatenate([mine, other]).reshape(-1, WIDTH)

    left = pl.BlockSpec(memory_space=pl.ANY)
    held = pl.pallas_call(
        gather_kernel,
        out_shape=jax.ShapeDtypeStruct((TOTAL, WIDTH), in_own.dtype),
        in_specs=[left] * 4,
        out_specs=pl.BlockSpec(memory_space=pltpu.VMEM),
        scratch_shapes=[pltpu.SemaphoreType.DMA((3 + features // WIDTH,))],
        cost_estimate=pl.CostEstimate(flops=0, bytes_accessed=6_000_000, transcendentals=0),
    )(in_own, down_own, saved_for(1), saved_for(-1))
    behind, ahead = shift_y(held, 1), shift_y(held, -1)

    arrive = shift_section(fwd_sent[0], 1)
    grad_back = shift_section(grad_sent[0], -1)
    wide, narrow = (BLOCK, features), (2 * BLOCK, features)
    send, table = call(
        pack_kernel,
        [(narrow, jnp.bfloat16), ((2 * BLOCK, 2 * BLOCK), jnp.bfloat16)],
        (route_fwd.reshape(1, BLOCK), route_bwd.reshape(1, BLOCK), arrive, grad_back, norm_gain, weight_bwd),
        traffic=2_000_000,
    )
    own = lax.cond(
        route_fwd[0, 0, 0] >= 0,
        exchange_z,
        exchange_halves,
        send.reshape(EXPERTS, 2 * CAP, features),
    )
    behind, ahead, saved_across = lax.optimization_barrier((behind, ahead, saved_for(2)))
    saved_across = shift_y(saved_across, 2)
    partner = swap_z(own)
    far_a = shift_y(behind[:FIRST], 1)
    far_b = shift_y(ahead[FIRST:NEXT], -1)
    rows = jnp.stack([own, partner]).reshape(2 * EXPERTS, 2, CAP, features)
    rows_fwd = rows[:, 0].reshape(-1, features)
    rows_bwd = rows[:, 1].reshape(-1, features)

    part, grad_part = call(
        near_kernel,
        [(narrow, jnp.float32)] * 2,
        (rows_fwd, rows_bwd, saved_for(0)),
        (in_own, down_own, behind, ahead),
        flops=2_100_000_000,
    )
    far = (far_a, far_b)
    (part,) = call(forward_kernel, [(narrow, jnp.bfloat16)], (rows_fwd, part), far, 350_000_000)
    received_fwd = swap_z(part[BLOCK:])
    (grad_part,) = call(backward_kernel, [(narrow, jnp.bfloat16)], (rows_bwd, grad_part, saved_across), far, 350_000_000)
    received_bwd = swap_z(grad_part[BLOCK:])

    def add(product, received):
        total = product[:BLOCK].astype(jnp.float32) + received.astype(jnp.float32)
        return total.astype(jnp.bfloat16).reshape(EXPERTS, CAP, features)

    sums = [add(part, received_fwd), add(grad_part, received_bwd)]
    back = exchange_z(jnp.concatenate(sums, axis=1)).reshape(narrow)
    forward_out, backward_out = call(
        finish_kernel,
        [(wide, jnp.bfloat16)] * 2,
        (table, back, arrive, grad_back, weight_fwd, saved_scale, norm_gain),
    )
    return (forward_out[None], backward_out[None])


def solution(mesh):
    in_specs = (
        P("section", "expert", None),
        P("section", "expert", None),
        P("section", "expert"),
        P("section", None),
        P("section", "expert", None, None),
        P("section", "expert", None, None),
        P("section", "expert", None, None),
        P("section", "expert", None),
        P("section", "expert", None),
        P("section", "expert"),
        P("section", "expert"),
    )
    out_specs = (P("section", "expert", None), P("section", "expert", None))
    return jax.shard_map(shards, mesh=mesh, in_specs=in_specs, out_specs=out_specs, check_vma=False)
```

time: 730 us -> 209 us (0.29)
  the two profiles are of different devices: /device:TPU:6 before, /device:TPU:26 now
where the time goes in v1:
time: 209 us
  blocking collectives  120 us (57%)
  waiting for transfers between devices  42.8 us (20%)
  starting transfers between devices  26.3 us (13%)
  Pallas kernels  14.5 us (7%)
  local copies, waits for them, and re-layouts  2.66 us (1%)
    all_to_all x2, blocking collectives, exchange_z(): lax.all_to_all(block, 'expert', split_axis=0, concat_axis=0, axis_index_g...  120 us
    ppermute x3, waiting for transfers between devices, swap_z(): return lax.ppermute(block, 'expert', [(k, k ^ ROWS) for k in range(size)])  24.2 us
    ppermute x5, starting transfers between devices, shift_y(): return lax.ppermute(block, 'expert', route)  15.1 us
    ppermute x5, waiting for transfers between devices, shift_y(): return lax.ppermute(block, 'expert', route)  12.3 us
    pallas_call x5, Pallas kernels, call(): pl.pallas_call(kernel, out_shape=[jax.ShapeDtypeStruct(shape, dtype) for...  11 us
    ppermute x3, starting transfers between devices, swap_z(): return lax.ppermute(block, 'expert', [(k, k ^ ROWS) for k in range(size)])  9.36 us
    ppermute x2, waiting for transfers between devices, shift_section(): lax.ppermute(block, 'section', [((i - distance) % size, i) for i in range...  6.32 us
  transfers between devices with their start and end apart: 10, of which 6 were waited for; matrix products, arithmetic and copies ran while one was open for 1% of the time, Pallas kernels for 4%

profile of v1, /device:TPU:26, one launch (start us, length us, event | category | flops | bytes accessed | tf_op | source)
XLA Modules:
  0.0 208.6 jit_solution(13571958721778206793)
XLA Ops:
  0.8 0.9 dynamic-slice_bitcast_fusion.1
  2.4 3.5 %shard_map.123 = bf16[5632,256]{1,0:T(8,128)(2,1)} custom-call(bf16[3584,256]{1,0:T(8,128)(2,1)} %bitcast.52, bf16[128,3584]{1,0:T(8,128)(2,1)} %bitcast.54, bf16[128,256]{1,0:T(8,128)(2,1)} %get-tuple-element.43.saved_next, bf16[128,256]{1,0:T(8,128)(2,1)} %get-tuple-element.44.saved_previous), custom_call_target="tpu_custom_call" | custom-call | bytes 6000000 | tf_op jit(solution)/shard_map/pallas_call | solution.py:247
  5.9 2.1 %collective-permute-start.3 = (bf16[5632,256]{1,0:T(8,128)(2,1)}, bf16[5632,256]{1,0:T(8,128)(2,1)S(1)}, u32[]{:S(2)}, u32[]{:S(2)}) collective-permute-start(bf16[5632,256]{1,0:T(8,128)(2,1)} %shard_map.123), channel_id=1, source_target_pairs={{0,1},{1,2},{2,3},{3,0},{4,5},{5,6},{6,7},{7,4},{8,9},{9,10},{10,1... | collective-permute-start | bytes 8650760 | tf_op jit(solution)/shard_map/ppermute | solution.py:32
  8.0 3.7 %collective-permute-start.4 = (bf16[5632,256]{1,0:T(8,128)(2,1)}, bf16[5632,256]{1,0:T(8,128)(2,1)}, u32[]{:S(2)}, u32[]{:S(2)}) collective-permute-start(bf16[5632,256]{1,0:T(8,128)(2,1)} %shard_map.123), channel_id=1, source_target_pairs={{0,3},{1,0},{2,1},{3,2},{4,7},{5,4},{6,5},{7,6},{8,11},{9,8},{10,9... | collective-permute-start | bytes 8650760 | tf_op jit(solution)/shard_map/ppermute | solution.py:32
  11.7 1.7 collective-permute-start.1
  13.5 6.3 %collective-permute-done.arrive = bf16[64,3584]{1,0:T(8,128)(2,1)S(1)} collective-permute-done((bf16[64,3584]{1,0:T(8,128)(2,1)}, bf16[64,3584]{1,0:T(8,128)(2,1)S(1)}, u32[]{:S(2)}, u32[]{:S(2)}) %collective-permute-start) | collective-permute-done | bytes 458784 | tf_op jit(solution)/shard_map/ppermute | solution.py:26
  20.6 59.9 %conditional.1 = (bf16[8,16,3584]{2,1,0:T(8,128)(2,1)}) conditional(s32[]{:T(128)} %bitcast.4, bf16[8,16,3584]{2,1,0:T(8,128)(2,1)S(1)} %bitcast.62, bf16[8,16,3584]{2,1,0:T(8,128)(2,1)S(1)} %bitcast.63), branch_computations={%region_0.1_spmd, %region_1.2_spmd} | conditional | flops 1835008 | bytes 5505032 | solution.py:266
  20.7 59.9 %all_to_all.19 = bf16[8,16,3584]{2,1,0:T(8,128)(2,1)} all-to-all(bf16[8,16,3584]{2,1,0:T(8,128)(2,1)S(1)} %param.1), channel_id=1, replica_groups={{0,8,16,24,32,40,48,56},{1,9,17,25,33,41,49,57},{2,10,18,26,34,42,50,58..., dimensions={0} | all-to-all | bytes 1835008 | tf_op jit(solution)/shard_map/cond/branch_1_fun/all_to_all | solution.py:42
  80.5 3.5 %collective-permute-start.2 = (bf16[8,16,3584]{2,1,0:T(8,128)(2,1)}, bf16[8,16,3584]{2,1,0:T(8,128)(2,1)S(1)}, u32[]{:S(2)}, u32[]{:S(2)}) collective-permute-start(bf16[8,16,3584]{2,1,0:T(8,128)(2,1)} %get-tuple-element.45), channel_id=1, source_target_pairs={{0,4},{1,5},{2,6},{3,7},{4,0},{5,1},{6,2},{7,3},{8,12},{9,13},{10,... | collective-permute-start | bytes 2752520 | tf_op jit(solution)/shard_map/ppermute | solution.py:37
  84.2 3.5 %collective-permute-start.5 = (bf16[2688,256]{1,0:T(8,128)(2,1)S(1)}, bf16[2688,256]{1,0:T(8,128)(2,1)S(1)}, u32[]{:S(2)}, u32[]{:S(2)}) collective-permute-start(bf16[2688,256]{1,0:T(8,128)(2,1)S(1)} %slice.36), channel_id=1, source_target_pairs={{0,1},{1,2},{2,3},{3,0},{4,5},{5,6},{6,7},{7,4},{8,9},{9,10},{10,1... | collective-permute-start | bytes 4128776 | tf_op jit(solution)/shard_map/ppermute | solution.py:32
  87.7 1.4 slice.37
  89.1 2.5 %collective-permute-start.6 = (bf16[2688,256]{1,0:T(8,128)(2,1)S(1)}, bf16[2688,256]{1,0:T(8,128)(2,1)S(1)}, u32[]{:S(2)}, u32[]{:S(2)}) collective-permute-start(bf16[2688,256]{1,0:T(8,128)(2,1)S(1)} %slice.37), channel_id=1, source_target_pairs={{0,3},{1,0},{2,1},{3,2},{4,7},{5,4},{6,5},{7,6},{8,11},{9,8},{10,9... | collective-permute-start | bytes 4128776 | tf_op jit(solution)/shard_map/ppermute | solution.py:32
  91.6 9.7 %collective-permute-done.2 = bf16[8,16,3584]{2,1,0:T(8,128)(2,1)S(1)} collective-permute-done((bf16[8,16,3584]{2,1,0:T(8,128)(2,1)}, bf16[8,16,3584]{2,1,0:T(8,128)(2,1)S(1)}, u32[]{:S(2)}, u32[]{:S(2)}) %collective-permute-start.2) | collective-permute-done | bytes 917536 | tf_op jit(solution)/shard_map/ppermute | solution.py:37
  101.6 3.3 %collective-permute-start.8 = (bf16[128,256]{1,0:T(8,128)(2,1)S(1)}, bf16[128,256]{1,0:T(8,128)(2,1)S(1)}, u32[]{:S(2)}, u32[]{:S(2)}) collective-permute-start(bf16[128,256]{1,0:T(8,128)(2,1)S(1)} %get-tuple-element.26), channel_id=1, source_target_pairs={{0,2},{1,3},{2,0},{3,1},{4,6},{5,7},{6,4},{7,5},{8,10},{9,11},{10,... | collective-permute-start | bytes 196616 | tf_op jit(solution)/shard_map/ppermute | solution.py:32
  105.0 5.4 %shard_map.124 = (f32[128,3584]{1,0:T(8,128)S(1)}, f32[128,3584]{1,0:T(8,128)S(1)}) custom-call(bf16[128,3584]{1,0:T(8,128)(2,1)S(1)} %get-tuple-element.31.rows_fwd.rows, bf16[128,3584]{1,0:T(8,128)(2,1)S(1)} %get-tuple-element.32.rows_bwd.rows, bf16[128,256]{1,0:T(8,128)(2,1)S(1)} %get-tuple-element.41.saved_own, bf16[3584,256]{1,0:T(8,128)(2,1)S(1)} %bitcast.53, ...), custom_call_target="tpu_custom_call" | custom-call | flops 2100000000 | bytes 8000000 | tf_op jit(solution)/shard_map/pallas_call | solution.py:208
  110.4 11.7 %collective-permute-done.8.saved = bf16[128,256]{1,0:T(8,128)(2,1)S(1)} collective-permute-done((bf16[128,256]{1,0:T(8,128)(2,1)S(1)}, bf16[128,256]{1,0:T(8,128)(2,1)S(1)}, u32[]{:S(2)}, u32[]{:S(2)}) %collective-permute-start.8) | collective-permute-done | bytes 65568 | tf_op jit(solution)/shard_map/ppermute | solution.py:32
  122.8 1.8 shard_map.126
  124.6 1.9 collective-permute-start.9
  126.5 1.7 shard_map.125
  128.3 3.9 %collective-permute-start.7 = (bf16[64,3584]{1,0:T(8,128)(2,1)S(1)}, bf16[64,3584]{1,0:T(8,128)(2,1)S(1)}, u32[]{:S(2)}, u32[]{:S(2)}) collective-permute-start(bf16[64,3584]{1,0:T(8,128)(2,1)S(1)} %slice.45), channel_id=1, source_target_pairs={{0,4},{1,5},{2,6},{3,7},{4,0},{5,1},{6,2},{7,3},{8,12},{9,13},{10,... | collective-permute-start | bytes 1376264 | tf_op jit(solution)/shard_map/ppermute | solution.py:37
  132.3 4.8 %collective-permute-done.9 = bf16[64,3584]{1,0:T(8,128)(2,1)S(1)} collective-permute-done((bf16[64,3584]{1,0:T(8,128)(2,1)S(1)}, bf16[64,3584]{1,0:T(8,128)(2,1)S(1)}, u32[]{:S(2)}, u32[]{:S(2)}) %collective-permute-start.9) | collective-permute-done | bytes 458784 | tf_op jit(solution)/shard_map/ppermute | solution.py:37
  137.2 9.7 %collective-permute-done.7 = bf16[64,3584]{1,0:T(8,128)(2,1)S(1)} collective-permute-done((bf16[64,3584]{1,0:T(8,128)(2,1)S(1)}, bf16[64,3584]{1,0:T(8,128)(2,1)S(1)}, u32[]{:S(2)}, u32[]{:S(2)}) %collective-permute-start.7) | collective-permute-done | bytes 458784 | tf_op jit(solution)/shard_map/ppermute | solution.py:37
  147.1 60.2 %all_to_all.20 = bf16[8,16,3584]{2,1,0:T(8,128)(2,1)S(1)} all-to-all(bf16[8,16,3584]{2,1,0:T(8,128)(2,1)S(1)} %pad_maximum_fusion.2), channel_id=1, replica_groups={{0,8,16,24,32,40,48,56},{1,9,17,25,33,41,49,57},{2,10,18,26,34,42,50,58..., dimensions={0} | all-to-all | bytes 1835008 | tf_op jit(solution)/shard_map/all_to_all | solution.py:42
  207.3 1.3 shard_map.127
  (39 shorter events, 2.9 us)
Async XLA Ops:
  2.3 11.1 %copy-start.5 = (s32[1,64,1]{1,2,0:T(1,128)S(1)}, s32[1,64,1]{1,2,0:T(1,128)}, u32[]{:S(2)}) copy-start(s32[1,64,1]{1,2,0:T(1,128)} %param.20) | copy-start | bytes 772
  2.3 17.5 %copy-start.4 = (f32[1,3584]{1,0:T(1,128)S(1)}, f32[1,3584]{1,0:T(1,128)}, u32[]{:S(2)}) copy-start(f32[1,3584]{1,0:T(1,128)} %gain.3) | copy-start | bytes 43012
  2.3 17.5 %copy-start.6 = (s32[1,64,1]{1,2,0:T(1,128)S(1)}, s32[1,64,1]{1,2,0:T(1,128)}, u32[]{:S(2)}) copy-start(s32[1,64,1]{1,2,0:T(1,128)} %param.21) | copy-start | bytes 772
  2.3 17.5 %copy-start.7 = (f32[1,64]{1,0:T(1,128)S(1)}, f32[1,64]{1,0:T(1,128)}, u32[]{:S(2)}) copy-start(f32[1,64]{1,0:T(1,128)} %weight.2) | copy-start | bytes 772
  5.9 78.2 %collective-permute-start.3 = (bf16[5632,256]{1,0:T(8,128)(2,1)}, bf16[5632,256]{1,0:T(8,128)(2,1)S(1)}, u32[]{:S(2)}, u32[]{:S(2)}) collective-permute-start(bf16[5632,256]{1,0:T(8,128)(2,1)} %shard_map.123), channel_id=1, source_target_pairs={{0,1},{1,2},{2,3},{3,0},{4,5},{5,6},{6,7},{7,4},{8,9},{9,10},{10,1... | collective-permute-start | bytes 8650760 | tf_op jit(solution)/shard_map/ppermute | solution.py:32
  8.0 76.1 %collective-permute-start.4 = (bf16[5632,256]{1,0:T(8,128)(2,1)}, bf16[5632,256]{1,0:T(8,128)(2,1)}, u32[]{:S(2)}, u32[]{:S(2)}) collective-permute-start(bf16[5632,256]{1,0:T(8,128)(2,1)} %shard_map.123), channel_id=1, source_target_pairs={{0,3},{1,0},{2,1},{3,2},{4,7},{5,4},{6,5},{7,6},{8,11},{9,8},{10,9... | collective-permute-start | bytes 8650760 | tf_op jit(solution)/shard_map/ppermute | solution.py:32
  11.7 8.1 %collective-permute-start = (bf16[64,3584]{1,0:T(8,128)(2,1)}, bf16[64,3584]{1,0:T(8,128)(2,1)S(1)}, u32[]{:S(2)}, u32[]{:S(2)}) collective-permute-start(bf16[64,3584]{1,0:T(8,128)(2,1)} %bitcast.66), channel_id=1, source_target_pairs={{448,0},{0,64},{64,128},{128,192},{192,256},{256,320},{320,384},{3... | collective-permute-start | bytes 1376264 | tf_op jit(solution)/shard_map/ppermute | solution.py:26
  11.7 8.1 %collective-permute-start.1 = (bf16[64,3584]{1,0:T(8,128)(2,1)}, bf16[64,3584]{1,0:T(8,128)(2,1)S(1)}, u32[]{:S(2)}, u32[]{:S(2)}) collective-permute-start(bf16[64,3584]{1,0:T(8,128)(2,1)} %bitcast.67), channel_id=1, source_target_pairs={{64,0},{128,64},{192,128},{256,192},{320,256},{384,320},{448,384},... | collective-permute-start | bytes 1376264 | tf_op jit(solution)/shard_map/ppermute | solution.py:26
  19.8 0.8 copy-start.2
  80.5 20.8 %collective-permute-start.2 = (bf16[8,16,3584]{2,1,0:T(8,128)(2,1)}, bf16[8,16,3584]{2,1,0:T(8,128)(2,1)S(1)}, u32[]{:S(2)}, u32[]{:S(2)}) collective-permute-start(bf16[8,16,3584]{2,1,0:T(8,128)(2,1)} %get-tuple-element.45), channel_id=1, source_target_pairs={{0,4},{1,5},{2,6},{3,7},{4,0},{5,1},{6,2},{7,3},{8,12},{9,13},{10,... | collective-permute-start | bytes 2752520 | tf_op jit(solution)/shard_map/ppermute | solution.py:37
  84.2 17.1 %copy-start.10 = (bf16[8,16,3584]{2,1,0:T(8,128)(2,1)S(1)}, bf16[8,16,3584]{2,1,0:T(8,128)(2,1)}, u32[]{:S(2)}) copy-start(bf16[8,16,3584]{2,1,0:T(8,128)(2,1)} %get-tuple-element.45) | copy-start | bytes 2752516
  84.2 37.9 %collective-permute-start.5 = (bf16[2688,256]{1,0:T(8,128)(2,1)S(1)}, bf16[2688,256]{1,0:T(8,128)(2,1)S(1)}, u32[]{:S(2)}, u32[]{:S(2)}) collective-permute-start(bf16[2688,256]{1,0:T(8,128)(2,1)S(1)} %slice.36), channel_id=1, source_target_pairs={{0,1},{1,2},{2,3},{3,0},{4,5},{5,6},{6,7},{7,4},{8,9},{9,10},{10,1... | collective-permute-start | bytes 4128776 | tf_op jit(solution)/shard_map/ppermute | solution.py:32
  89.1 33.6 %collective-permute-start.6 = (bf16[2688,256]{1,0:T(8,128)(2,1)S(1)}, bf16[2688,256]{1,0:T(8,128)(2,1)S(1)}, u32[]{:S(2)}, u32[]{:S(2)}) collective-permute-start(bf16[2688,256]{1,0:T(8,128)(2,1)S(1)} %slice.37), channel_id=1, source_target_pairs={{0,3},{1,0},{2,1},{3,2},{4,7},{5,4},{6,5},{7,6},{8,11},{9,8},{10,9... | collective-permute-start | bytes 4128776 | tf_op jit(solution)/shard_map/ppermute | solution.py:32
  101.5 3.5 %copy-start = (bf16[1,1,3584,256]{3,2,1,0:T(8,128)(2,1)S(1)}, bf16[1,1,3584,256]{3,2,1,0:T(8,128)(2,1)}, u32[]{:S(2)}) copy-start(bf16[1,1,3584,256]{3,2,1,0:T(8,128)(2,1)} %param.17) | copy-start | bytes 5505028
  101.5 3.5 %copy-start.1 = (bf16[1,1,128,3584]{3,2,1,0:T(8,128)(2,1)S(1)}, bf16[1,1,128,3584]{3,2,1,0:T(8,128)(2,1)}, u32[]{:S(2)}) copy-start(bf16[1,1,128,3584]{3,2,1,0:T(8,128)(2,1)} %param.18) | copy-start | bytes 2752516
  101.6 20.5 %collective-permute-start.8 = (bf16[128,256]{1,0:T(8,128)(2,1)S(1)}, bf16[128,256]{1,0:T(8,128)(2,1)S(1)}, u32[]{:S(2)}, u32[]{:S(2)}) collective-permute-start(bf16[128,256]{1,0:T(8,128)(2,1)S(1)} %get-tuple-element.26), channel_id=1, source_target_pairs={{0,2},{1,3},{2,0},{3,1},{4,6},{5,7},{6,4},{7,5},{8,10},{9,11},{10,... | collective-permute-start | bytes 196616 | tf_op jit(solution)/shard_map/ppermute | solution.py:32
  124.6 12.4 %collective-permute-start.9 = (bf16[64,3584]{1,0:T(8,128)(2,1)S(1)}, bf16[64,3584]{1,0:T(8,128)(2,1)S(1)}, u32[]{:S(2)}, u32[]{:S(2)}) collective-permute-start(bf16[64,3584]{1,0:T(8,128)(2,1)S(1)} %slice.47), channel_id=1, source_target_pairs={{0,4},{1,5},{2,6},{3,7},{4,0},{5,1},{6,2},{7,3},{8,12},{9,13},{10,... | collective-permute-start | bytes 1376264 | tf_op jit(solution)/shard_map/ppermute | solution.py:37
  128.3 18.5 %collective-permute-start.7 = (bf16[64,3584]{1,0:T(8,128)(2,1)S(1)}, bf16[64,3584]{1,0:T(8,128)(2,1)S(1)}, u32[]{:S(2)}, u32[]{:S(2)}) collective-permute-start(bf16[64,3584]{1,0:T(8,128)(2,1)S(1)} %slice.45), channel_id=1, source_target_pairs={{0,4},{1,5},{2,6},{3,7},{4,0},{5,1},{6,2},{7,3},{8,12},{9,13},{10,... | collective-permute-start | bytes 1376264 | tf_op jit(solution)/shard_map/ppermute | solution.py:37
  147.0 60.3 %copy-start.3 = (bf16[64,3584]{1,0:T(8,128)(2,1)S(1)}, bf16[64,3584]{1,0:T(8,128)(2,1)}, u32[]{:S(2)}) copy-start(bf16[64,3584]{1,0:T(8,128)(2,1)} %copy-done.2) | copy-start | bytes 1376260
  147.0 60.3 %copy-start.8 = (f32[1,64]{1,0:T(1,128)S(1)}, f32[1,64]{1,0:T(1,128)}, u32[]{:S(2)}) copy-start(f32[1,64]{1,0:T(1,128)} %weight.3) | copy-start | bytes 772
  147.0 60.3 %copy-start.9 = (f32[1,64]{1,0:T(1,128)S(1)}, f32[1,64]{1,0:T(1,128)}, u32[]{:S(2)}) copy-start(f32[1,64]{1,0:T(1,128)} %scale.1) | copy-start | bytes 772

commit v2 on v1

--- a/solution.py
+++ b/solution.py
@@ -11,11 +11,13 @@
 BLOCK = EXPERTS * CAP
 EPSILON = 1e-06
 
-FIRST = 2688
-LAST = 896
-DOWN = FIRST + LAST
-NEXT = 2 * FIRST
+FIRST = 1792
+LAST = 1792
+PART = 8
+ACROSS = 1792
+NEXT = ACROSS + 128
 TOTAL = NEXT + 256
+CHUNKS = ((0, 896), (896, 896), (FIRST, 896), (FIRST + 896, 896))
 WIDTH = 256
 HIDDEN = 128
 VMEM_LIMIT = 40 * 1024 * 1024
@@ -42,10 +44,6 @@
     return lax.all_to_all(
         block, "expert", split_axis=0, concat_axis=0, axis_index_groups=groups, tiled=True
     )
-
-
-def exchange_halves(block):
-    return jnp.concatenate([exchange_z(block[:, :CAP]), exchange_z(block[:, CAP:])], axis=1)
 
 
 def as_column(row):
@@ -56,10 +54,10 @@
     return jnp.sum(spread, axis=1, keepdims=True)
 
 
-def pack_kernel(route_fwd, route_bwd, arrive, grad_back, gain, weight, send, table):
-    chosen = jnp.concatenate(
-        [as_column(route[...].astype(jnp.float32)) for route in (route_fwd, route_bwd)], axis=0
-    )
+def pack_kernel(values, arrive, grad_back, send, table):
+    features = arrive.shape[1]
+    chosen = as_column(values[:, features : features + 128])
+    weights = as_column(values[:, features + 128 : features + 256])
     shape = (2 * BLOCK, 2 * BLOCK)
     token = lax.broadcasted_iota(jnp.int32, shape, 0)
     column = lax.broadcasted_iota(jnp.int32, shape, 1)
@@ -71,35 +69,37 @@
     table[...] = onehot
     wide = arrive[...].astype(jnp.float32)
     inverse = lax.rsqrt(jnp.mean(wide * wide, axis=-1, keepdims=True) + EPSILON)
-    normed = (wide * inverse * gain[...]).astype(jnp.bfloat16)
-    scaled = (grad_back[...].astype(jnp.float32) * as_column(weight[...])).astype(jnp.bfloat16)
+    normed = (wide * inverse * values[:, :features]).astype(jnp.bfloat16)
+    scaled = (grad_back[...].astype(jnp.float32) * weights[BLOCK:]).astype(jnp.bfloat16)
     tokens = jnp.concatenate([normed, scaled], axis=0)
     send[...] = lax.dot_general(
         onehot, tokens, (((0,), (0,)), ((), ())), preferred_element_type=jnp.float32
     ).astype(send.dtype)
 
 
-def finish_kernel(table, back, arrive, grad_back, weight, scale, gain, forward_out, backward_out):
+def finish_kernel(values, table, back, arrive, grad_back, forward_out, backward_out):
+    features = arrive.shape[1]
+    weights = as_column(values[:, features + 128 : features + 256])
+    scales = as_column(values[:, features + 256 :])
     got = mm(table[...], back[...])
     wide = arrive[...].astype(jnp.float32)
-    forward_out[...] = (wide + as_column(weight[...]) * got[:BLOCK]).astype(forward_out.dtype)
+    forward_out[...] = (wide + weights[:BLOCK] * got[:BLOCK]).astype(forward_out.dtype)
     back_wide = grad_back[...].astype(jnp.float32)
-    grad_start = as_column(scale[...]) * gain[...] * got[BLOCK:]
+    grad_start = scales[BLOCK:] * values[:, :features] * got[BLOCK:]
     backward_out[...] = (back_wide + grad_start).astype(backward_out.dtype)
 
 
-def gather_kernel(in_own, down_own, saved_next, saved_previous, held, sems):
-    count = down_own.shape[1] // WIDTH
+def gather_kernel(down_own, saved_across, saved_next, saved_previous, held, sems):
     pieces = [
-        (in_own, held.at[pl.ds(0, DOWN)]),
+        (saved_across, held.at[pl.ds(ACROSS, 128)]),
         (saved_next, held.at[pl.ds(NEXT, 128)]),
         (saved_previous, held.at[pl.ds(NEXT + 128, 128)]),
     ]
-    for c in range(count):
+    for c in range(down_own.shape[1] // WIDTH):
         pieces.append(
             (
                 down_own.at[:, pl.ds(c * WIDTH, WIDTH)],
-                held.at[pl.ds(DOWN + c * HIDDEN, HIDDEN)],
+                held.at[pl.ds(c * HIDDEN, HIDDEN)],
             )
         )
     copies = [pltpu.make_async_copy(p[0], p[1], sems.at[i]) for i, p in enumerate(pieces)]
@@ -129,13 +129,23 @@
     return (gate / (1.0 + jnp.exp(-gate)) * up).astype(jnp.bfloat16)
 
 
-def slope(grad_act, saved):
+def factors(saved):
     wide = saved.astype(jnp.float32)
     gate, up = wide[:, :HIDDEN], wide[:, HIDDEN:]
     sigmoid = 1.0 / (1.0 + jnp.exp(-gate))
-    grad_gate = grad_act * up * sigmoid * (1.0 + gate * (1.0 - sigmoid))
-    grad_up = grad_act * gate * sigmoid
-    return jnp.concatenate([grad_gate, grad_up], axis=1).astype(jnp.bfloat16)
+    return up * sigmoid * (1.0 + gate * (1.0 - sigmoid)), gate * sigmoid
+
+
+def slope(grad_act, gate_factor, up_factor):
+    return jnp.concatenate([grad_act * gate_factor, grad_act * up_factor], axis=1).astype(
+        jnp.bfloat16
+    )
+
+
+def factor_kernel(own, behind, ahead, out):
+    for i, saved in enumerate((own, behind, ahead)):
+        rows = slice(i * 128, (i + 1) * 128)
+        out[rows, :HIDDEN], out[rows, HIDDEN:] = factors(saved[...])
 
 
 def down_blocks(held, start, count):
@@ -150,55 +160,79 @@
     return total
 
 
-def near_kernel(rows_fwd, rows_bwd, saved_own, *refs):
-    sources, part, grad_part, buffers, sems = refs[:4], refs[4], refs[5], refs[6:10], refs[10]
+def near_kernel(rows_fwd, rows_bwd, factor, *refs):
+    sources, part, grad_part, buffers, sems = refs[:6], refs[6], refs[7], refs[8:14], refs[14]
     copies = fetch(sources, buffers, sems)
-    own_in, own_down, behind, ahead = buffers
+    own_in, own_down, behind_in, behind, ahead_in, ahead = buffers
     count = rows_fwd.shape[1] // WIDTH
+
+    def scaled(i, grad_act):
+        rows = slice(i * 128, (i + 1) * 128)
+        return slope(grad_act, factor[rows, :HIDDEN], factor[rows, HIDDEN:])
+
     copies[0].wait()
     copies[1].wait()
     acts = [activate(mm(rows_fwd[...], own_in[...]))]
-    grads = [slope(mt(rows_bwd[...], own_down[...]), saved_own[...])]
-    for i, near, saved in ((2, behind, NEXT), (3, ahead, NEXT + 128)):
-        copies[i].wait()
-        acts.append(activate(mm(rows_fwd[...], near[:DOWN])))
-        grads.append(slope(across_blocks(rows_bwd, near, DOWN), near[saved : saved + 128]))
+    grads = [scaled(0, mt(rows_bwd[...], own_down[...]))]
+    for i, near_in, near in ((1, behind_in, behind), (2, ahead_in, ahead)):
+        copies[2 * i].wait()
+        copies[2 * i + 1].wait()
+        acts.append(activate(mm(rows_fwd[...], near_in[...])))
+        grads.append(scaled(i, across_blocks(rows_bwd, near, 0)))
     for c in range(count):
         columns = slice(c * WIDTH, (c + 1) * WIDTH)
-        block = slice(DOWN + c * HIDDEN, DOWN + (c + 1) * HIDDEN)
+        block = slice(c * HIDDEN, (c + 1) * HIDDEN)
         total = mm(acts[0], own_down[:, columns])
         part[:, columns] = total + mm(acts[1], behind[block]) + mm(acts[2], ahead[block])
-    for c in range(count * WIDTH // LAST):
-        columns = slice(c * LAST, (c + 1) * LAST)
+    for start, size in CHUNKS:
+        columns = slice(start, start + size)
         total = mt(grads[0], own_in[columns])
-        grad_part[:, columns] = total + mt(grads[1], behind[columns]) + mt(grads[2], ahead[columns])
+        total += mt(grads[1], behind_in[columns]) + mt(grads[2], ahead_in[columns])
+        grad_part[:, columns] = total
 
 
 def forward_kernel(rows, part, *refs):
-    sources, out, buffers, sems = refs[:2], refs[2], refs[3:5], refs[5]
+    sources, out, buffers, sems = refs[:4], refs[4], refs[5:9], refs[9]
     copies = fetch(sources, buffers, sems)
-    far_a, far_b = buffers
+    first, last, down_first, down_last = buffers
     copies[0].wait()
-    pre = mm(rows[:, :FIRST], far_a[...])
+    pre = mm(rows[:, :FIRST], first[...])
     copies[1].wait()
-    act = activate(pre + mm(rows[:, FIRST:], far_b[:LAST]))
+    act = activate(pre + mm(rows[:, FIRST:], last[...]))
+    copies[2].wait()
+    copies[3].wait()
     count = rows.shape[1] // WIDTH
-    for c, block in enumerate(down_blocks(far_b, LAST, count)):
+    blocks = down_blocks(down_first, 0, PART) + down_blocks(down_last, 0, count - PART)
+    for c, block in enumerate(blocks):
         columns = slice(c * WIDTH, (c + 1) * WIDTH)
         out[:, columns] = (part[:, columns] + mm(act, block)).astype(out.dtype)
 
 
-def backward_kernel(rows, part, saved, *refs):
-    sources, out, buffers, sems = refs[:2], refs[2], refs[3:5], refs[5]
+def backward_kernel(rows, part, *refs):
+    sources, out, buffers, sems = refs[:4], refs[4], refs[5:9], refs[9]
     copies = fetch(sources, buffers, sems)
-    far_a, far_b = buffers
+    first, last, down_first, down_last = buffers
+    copies[2].wait()
+    copies[3].wait()
+    middle = PART * WIDTH
+    grad_act = across_blocks(rows[:, :middle], down_first, 0)
+    grad_act += across_blocks(rows[:, middle:], down_last, 0)
+    grad = slope(grad_act, *factors(down_last[ACROSS - PART * HIDDEN :]))
     copies[0].wait()
     copies[1].wait()
-    grad = slope(across_blocks(rows, far_b, LAST), saved[...])
-    for c in range(rows.shape[1] // LAST):
-        columns = slice(c * LAST, (c + 1) * LAST)
-        weights = far_a[columns] if c * LAST < FIRST else far_b[:LAST]
+    for start, size in CHUNKS:
+        columns = slice(start, start + size)
+        weights = first[columns] if start < FIRST else last[start - FIRST : start - FIRST + size]
         out[:, columns] = (part[:, columns] + mt(grad, weights)).astype(out.dtype)
+
+
+def halves_kernel(behind, ahead, first, last, sems):
+    one = pltpu.make_async_copy(behind.at[pl.ds(0, FIRST)], first, sems.at[0])
+    two = pltpu.make_async_copy(ahead.at[pl.ds(FIRST, LAST)], last, sems.at[1])
+    one.start()
+    two.start()
+    one.wait()
+    two.wait()
 
 
 def call(kernel, outs, whole, held=(), flops=0, traffic=8_000_000):
@@ -250,30 +284,49 @@
         in_specs=[left] * 4,
         out_specs=pl.BlockSpec(memory_space=pltpu.VMEM),
         scratch_shapes=[pltpu.SemaphoreType.DMA((3 + features // WIDTH,))],
-        cost_estimate=pl.CostEstimate(flops=0, bytes_accessed=6_000_000, transcendentals=0),
-    )(in_own, down_own, saved_for(1), saved_for(-1))
+        cost_estimate=pl.CostEstimate(flops=0, bytes_accessed=2_000_000, transcendentals=0),
+    )(down_own, saved_for(2), saved_for(1), saved_for(-1))
+    behind_in, ahead_in = shift_y(in_own, 1), shift_y(in_own, -1)
     behind, ahead = shift_y(held, 1), shift_y(held, -1)
 
+    routes = [route.reshape(1, BLOCK).astype(jnp.float32) for route in (route_fwd, route_bwd)]
+    values = jnp.concatenate(
+        [norm_gain, *routes, weight_fwd, weight_bwd, saved_scale, saved_scale], axis=1
+    )
     arrive = shift_section(fwd_sent[0], 1)
     grad_back = shift_section(grad_sent[0], -1)
     wide, narrow = (BLOCK, features), (2 * BLOCK, features)
     send, table = call(
         pack_kernel,
         [(narrow, jnp.bfloat16), ((2 * BLOCK, 2 * BLOCK), jnp.bfloat16)],
-        (route_fwd.reshape(1, BLOCK), route_bwd.reshape(1, BLOCK), arrive, grad_back, norm_gain, weight_bwd),
-        traffic=2_000_000,
-    )
-    own = lax.cond(
-        route_fwd[0, 0, 0] >= 0,
-        exchange_z,
-        exchange_halves,
-        send.reshape(EXPERTS, 2 * CAP, features),
-    )
-    behind, ahead, saved_across = lax.optimization_barrier((behind, ahead, saved_for(2)))
-    saved_across = shift_y(saved_across, 2)
+        (values, arrive, grad_back),
+        flops=20_000_000_000,
+    )
+    own = exchange_z(send.reshape(EXPERTS, 2 * CAP, features))
+    halves = pl.pallas_call(
+        halves_kernel,
+        out_shape=[jax.ShapeDtypeStruct((n, WIDTH), in_own.dtype) for n in (FIRST, LAST)],
+        in_specs=[left] * 2,
+        out_specs=[pl.BlockSpec(memory_space=pltpu.VMEM)] * 2,
+        scratch_shapes=[pltpu.SemaphoreType.DMA((2,))],
+        cost_estimate=pl.CostEstimate(flops=20_000_000_000, bytes_accessed=4_000_000, transcendentals=0),
+    )(behind_in, ahead_in)
+    far_in = (shift_y(halves[0], 1), shift_y(halves[1], -1))
     partner = swap_z(own)
-    far_a = shift_y(behind[:FIRST], 1)
-    far_b = shift_y(ahead[FIRST:NEXT], -1)
+    far_in, partner, saved_behind = lax.optimization_barrier(
+        (far_in, partner, behind[NEXT : NEXT + 128])
+    )
+    (factor,) = call(
+        factor_kernel,
+        [((384, WIDTH), jnp.float32)],
+        (saved_for(0), saved_behind, ahead[NEXT + 128 :]),
+        flops=1_000_000_000,
+    )
+    far_down = (
+        shift_y(behind[: PART * HIDDEN], 1),
+        shift_y(ahead[PART * HIDDEN : NEXT], -1),
+    )
+    far = (*far_in, *far_down)
     rows = jnp.stack([own, partner]).reshape(2 * EXPERTS, 2, CAP, features)
     rows_fwd = rows[:, 0].reshape(-1, features)
     rows_bwd = rows[:, 1].reshape(-1, features)
@@ -281,14 +334,14 @@
     part, grad_part = call(
         near_kernel,
         [(narrow, jnp.float32)] * 2,
-        (rows_fwd, rows_bwd, saved_for(0)),
-        (in_own, down_own, behind, ahead),
-        flops=2_100_000_000,
-    )
-    far = (far_a, far_b)
+        (rows_fwd, rows_bwd, factor),
+        (in_own, down_own, behind_in, behind, ahead_in, ahead),
+        flops=2_000_000_000,
+        traffic=0,
+    )
     (part,) = call(forward_kernel, [(narrow, jnp.bfloat16)], (rows_fwd, part), far, 350_000_000)
     received_fwd = swap_z(part[BLOCK:])
-    (grad_part,) = call(backward_kernel, [(narrow, jnp.bfloat16)], (rows_bwd, grad_part, saved_across), far, 350_000_000)
+    (grad_part,) = call(backward_kernel, [(narrow, jnp.bfloat16)], (rows_bwd, grad_part), far, 350_000_000)
     received_bwd = swap_z(grad_part[BLOCK:])
 
     def add(product, received):
@@ -300,7 +353,7 @@
     forward_out, backward_out = call(
         finish_kernel,
         [(wide, jnp.bfloat16)] * 2,
-        (table, back, arrive, grad_back, weight_fwd, saved_scale, norm_gain),
+        (values, table, back, arrive, grad_back),
     )
     return (forward_out[None], backward_out[None])
 

time: 209 us -> 190 us (0.909)
  the two profiles are of different devices: /device:TPU:26 before, /device:TPU:90 now
where the time goes in v2:
time: 190 us; the launch traced here: 189 us
  waiting for transfers between devices  60.1 us (32%)
  blocking collectives  53.8 us (28%)
  starting transfers between devices  47.7 us (25%)
  Pallas kernels  18.1 us (10%)
  local copies, waits for them, and re-layouts  5.12 us (3%)
  other arithmetic  3.6 us (2%)
    all_to_all x1, blocking collectives, exchange_z(): lax.all_to_all(block, 'expert', split_axis=0, concat_axis=0, axis_index_g...  53.8 us
    ppermute x8, waiting for transfers between devices, shift_y(): return lax.ppermute(block, 'expert', route)  24 us
    ppermute x8, starting transfers between devices, shift_y(): return lax.ppermute(block, 'expert', route)  23.4 us
    ppermute x3, waiting for transfers between devices, swap_z(): return lax.ppermute(block, 'expert', [(k, k ^ ROWS) for k in range(size)])  20.1 us
    all_to_all x1, waiting for transfers between devices, exchange_z(): lax.all_to_all(block, 'expert', split_axis=0, concat_axis=0, axis_index_g...  16 us
    all_to_all x1, starting transfers between devices, exchange_z(): lax.all_to_all(block, 'expert', split_axis=0, concat_axis=0, axis_index_g...  14.9 us
    pallas_call x6, Pallas kernels, call(): pl.pallas_call(kernel, out_shape=[jax.ShapeDtypeStruct(shape, dtype) for...  12.9 us
    ppermute x3, starting transfers between devices, swap_z(): return lax.ppermute(block, 'expert', [(k, k ^ ROWS) for k in range(size)])  7.75 us
  transfers between devices with their start and end apart: 14, of which 8 were waited for; matrix products, arithmetic and copies ran while one was open for 3% of the time, Pallas kernels for 8%

profile of v2, /device:TPU:90, one launch (start us, length us, event | category | flops | bytes accessed | tf_op | source)
XLA Modules:
  0.0 189.4 jit_solution(12973780770212891156)
XLA Ops:
  2.4 2.1 %collective-permute-start.2 = (bf16[3584,256]{1,0:T(8,128)(2,1)}, bf16[3584,256]{1,0:T(8,128)(2,1)S(1)}, u32[]{:S(2)}, u32[]{:S(2)}) collective-permute-start(bf16[3584,256]{1,0:T(8,128)(2,1)} %bitcast.51), channel_id=1, source_target_pairs={{0,1},{1,2},{2,3},{3,0},{4,5},{5,6},{6,7},{7,4},{8,9},{9,10},{10,1... | collective-permute-start | bytes 5505032 | tf_op jit(solution)/shard_map/ppermute | solution.py:34
  4.5 3.7 %collective-permute-start.3 = (bf16[3584,256]{1,0:T(8,128)(2,1)}, bf16[3584,256]{1,0:T(8,128)(2,1)}, u32[]{:S(2)}, u32[]{:S(2)}) collective-permute-start(bf16[3584,256]{1,0:T(8,128)(2,1)} %bitcast.52), channel_id=1, source_target_pairs={{0,3},{1,0},{2,1},{3,2},{4,7},{5,4},{6,5},{7,6},{8,11},{9,8},{10,9... | collective-permute-start | bytes 5505032 | tf_op jit(solution)/shard_map/ppermute | solution.py:34
  11.4 14.9 %all-to-all-start = ((bf16[8,16,3584]{2,1,0:T(8,128)(2,1)}), bf16[8,16,3584]{2,1,0:T(8,128)(2,1)}, u32[]{:S(2)}, u32[]{:S(2)}) async-start(bf16[8,16,3584]{2,1,0:T(8,128)(2,1)} %bitcast.4), calls=%async_computation | async-start | bytes 1835008 | tf_op jit(solution)/shard_map/all_to_all | solution.py:44
  27.6 2.4 %shard_map.124 = bf16[2176,256]{1,0:T(8,128)(2,1)} custom-call(bf16[128,3584]{1,0:T(8,128)(2,1)} %bitcast.49, bf16[128,256]{1,0:T(8,128)(2,1)} %get-tuple-element.38.saved_across, bf16[128,256]{1,0:T(8,128)(2,1)} %get-tuple-element.39.saved_next, bf16[128,256]{1,0:T(8,128)(2,1)} %maximum_bitcast_fusion.2.saved_previous), custom_call_target="tpu_custom_call" | custom-call | bytes 2000000 | tf_op jit(solution)/shard_map/pallas_call | solution.py:281
  30.0 3.3 %collective-permute-start.7 = (bf16[2176,256]{1,0:T(8,128)(2,1)}, bf16[2176,256]{1,0:T(8,128)(2,1)S(1)}, u32[]{:S(2)}, u32[]{:S(2)}) collective-permute-start(bf16[2176,256]{1,0:T(8,128)(2,1)} %shard_map.124), channel_id=1, source_target_pairs={{0,1},{1,2},{2,3},{3,0},{4,5},{5,6},{6,7},{7,4},{8,9},{9,10},{10,1... | collective-permute-start | bytes 3342344 | tf_op jit(solution)/shard_map/ppermute | solution.py:34
  33.4 2.5 %collective-permute-start.8 = (bf16[2176,256]{1,0:T(8,128)(2,1)}, bf16[2176,256]{1,0:T(8,128)(2,1)}, u32[]{:S(2)}, u32[]{:S(2)}) collective-permute-start(bf16[2176,256]{1,0:T(8,128)(2,1)} %shard_map.124), channel_id=1, source_target_pairs={{0,3},{1,0},{2,1},{3,2},{4,7},{5,4},{6,5},{7,6},{8,11},{9,8},{10,9... | collective-permute-start | bytes 3342344 | tf_op jit(solution)/shard_map/ppermute | solution.py:34
  35.9 11.5 %collective-permute-done.2.behind.refs_2_ = bf16[3584,256]{1,0:T(8,128)(2,1)S(1)} collective-permute-done((bf16[3584,256]{1,0:T(8,128)(2,1)}, bf16[3584,256]{1,0:T(8,128)(2,1)S(1)}, u32[]{:S(2)}, u32[]{:S(2)}) %collective-permute-start.2) | collective-permute-done | bytes 1835040 | tf_op jit(solution)/shard_map/ppermute | solution.py:34
  47.4 3.5 %collective-permute-done.3.ahead.refs_4_ = bf16[3584,256]{1,0:T(8,128)(2,1)} collective-permute-done((bf16[3584,256]{1,0:T(8,128)(2,1)}, bf16[3584,256]{1,0:T(8,128)(2,1)}, u32[]{:S(2)}, u32[]{:S(2)}) %collective-permute-start.3) | collective-permute-done | bytes 1835040 | tf_op jit(solution)/shard_map/ppermute | solution.py:34
  50.9 2.8 %shard_map.123 = (bf16[1792,256]{1,0:T(8,128)(2,1)}, bf16[1792,256]{1,0:T(8,128)(2,1)}) custom-call(bf16[3584,256]{1,0:T(8,128)(2,1)} %copy-done.2, bf16[3584,256]{1,0:T(8,128)(2,1)} %collective-permute-done.3.ahead.refs_4_), custom_call_target="tpu_custom_call" | custom-call | flops 20000000000 | bytes 4000000 | tf_op jit(solution)/shard_map/pallas_call | solution.py:306
  53.7 2.3 %collective-permute-start.4 = (bf16[1792,256]{1,0:T(8,128)(2,1)}, bf16[1792,256]{1,0:T(8,128)(2,1)S(1)}, u32[]{:S(2)}, u32[]{:S(2)}) collective-permute-start(bf16[1792,256]{1,0:T(8,128)(2,1)} %get-tuple-element.16), channel_id=1, source_target_pairs={{0,1},{1,2},{2,3},{3,0},{4,5},{5,6},{6,7},{7,4},{8,9},{9,10},{10,1... | collective-permute-start | bytes 2752520 | tf_op jit(solution)/shard_map/ppermute | solution.py:34
  56.0 3.6 %collective-permute-start.5 = (bf16[1792,256]{1,0:T(8,128)(2,1)}, bf16[1792,256]{1,0:T(8,128)(2,1)S(1)}, u32[]{:S(2)}, u32[]{:S(2)}) collective-permute-start(bf16[1792,256]{1,0:T(8,128)(2,1)} %get-tuple-element.17), channel_id=1, source_target_pairs={{0,3},{1,0},{2,1},{3,2},{4,7},{5,4},{6,5},{7,6},{8,11},{9,8},{10,9... | collective-permute-start | bytes 2752520 | tf_op jit(solution)/shard_map/ppermute | solution.py:34
  59.5 16.0 %all-to-all-done = bf16[8,16,3584]{2,1,0:T(8,128)(2,1)} async-done(((bf16[8,16,3584]{2,1,0:T(8,128)(2,1)}), bf16[8,16,3584]{2,1,0:T(8,128)(2,1)}, u32[]{:S(2)}, u32[]{:S(2)}) %all-to-all-start) | async-done | bytes 917536 | tf_op jit(solution)/shard_map/all_to_all | solution.py:44
  80.6 3.7 %collective-permute-start.10 = (bf16[896,256]{1,0:T(8,128)(2,1)S(1)}, bf16[896,256]{1,0:T(8,128)(2,1)S(1)}, u32[]{:S(2)}, u32[]{:S(2)}) collective-permute-start(bf16[896,256]{1,0:T(8,128)(2,1)S(1)} %slice.45), channel_id=1, source_target_pairs={{0,3},{1,0},{2,1},{3,2},{4,7},{5,4},{6,5},{7,6},{8,11},{9,8},{10,9... | collective-permute-start | bytes 1376264 | tf_op jit(solution)/shard_map/ppermute | solution.py:34
  85.3 5.7 %collective-permute-done.4.refs_0_ = bf16[1792,256]{1,0:T(8,128)(2,1)S(1)} collective-permute-done((bf16[1792,256]{1,0:T(8,128)(2,1)}, bf16[1792,256]{1,0:T(8,128)(2,1)S(1)}, u32[]{:S(2)}, u32[]{:S(2)}) %collective-permute-start.4) | collective-permute-done | bytes 917536 | tf_op jit(solution)/shard_map/ppermute | solution.py:34
  90.9 3.4 %collective-permute-done.5.refs_1_ = bf16[1792,256]{1,0:T(8,128)(2,1)S(1)} collective-permute-done((bf16[1792,256]{1,0:T(8,128)(2,1)}, bf16[1792,256]{1,0:T(8,128)(2,1)S(1)}, u32[]{:S(2)}, u32[]{:S(2)}) %collective-permute-start.5) | collective-permute-done | bytes 917536 | tf_op jit(solution)/shard_map/ppermute | solution.py:34
  94.3 5.3 %collective-permute-done.6 = bf16[8,16,3584]{2,1,0:T(8,128)(2,1)S(1)} collective-permute-done((bf16[8,16,3584]{2,1,0:T(8,128)(2,1)}, bf16[8,16,3584]{2,1,0:T(8,128)(2,1)S(1)}, u32[]{:S(2)}, u32[]{:S(2)}) %collective-permute-start.6) | collective-permute-done | bytes 917536 | tf_op jit(solution)/shard_map/ppermute | solution.py:39
  103.3 5.5 %shard_map.126 = (f32[128,3584]{1,0:T(8,128)S(1)}, f32[128,3584]{1,0:T(8,128)S(1)}) custom-call(bf16[128,3584]{1,0:T(8,128)(2,1)S(1)} %get-tuple-element.26.rows_fwd.rows, bf16[128,3584]{1,0:T(8,128)(2,1)S(1)} %get-tuple-element.27.rows_bwd.rows, f32[384,256]{1,0:T(8,128)S(1)} %shard_map.125.factor, bf16[3584,256]{1,0:T(8,128)(2,1)S(1)} %bitcast.53, ...), custom_call_target="tpu_custom_call" | custom-call | flops 2000000000 | tf_op jit(solution)/shard_map/pallas_call | solution.py:242
  108.8 2.3 %shard_map.128 = bf16[128,3584]{1,0:T(8,128)(2,1)S(1)} custom-call(bf16[128,3584]{1,0:T(8,128)(2,1)S(1)} %get-tuple-element.27.rows_bwd.rows, f32[128,3584]{1,0:T(8,128)S(1)} %get-tuple-element.23.part, bf16[1792,256]{1,0:T(8,128)(2,1)S(1)} %collective-permute-done.4.refs_0_, bf16[1792,256]{1,0:T(8,128)(2,1)S(1)} %collective-permute-done.5.refs_1_, ...), custom_call_target="tpu_custom_call" | custom-call | flops 350000000 | bytes 8000000 | tf_op jit(solution)/shard_map/pallas_call | solution.py:242
  111.2 2.2 %collective-permute-start.12 = (bf16[64,3584]{1,0:T(8,128)(2,1)S(1)}, bf16[64,3584]{1,0:T(8,128)(2,1)S(1)}, u32[]{:S(2)}, u32[]{:S(2)}) collective-permute-start(bf16[64,3584]{1,0:T(8,128)(2,1)S(1)} %slice.49), channel_id=1, source_target_pairs={{0,4},{1,5},{2,6},{3,7},{4,0},{5,1},{6,2},{7,3},{8,12},{9,13},{10,... | collective-permute-start | bytes 1376264 | tf_op jit(solution)/shard_map/ppermute | solution.py:39
  113.4 2.1 %shard_map.127 = bf16[128,3584]{1,0:T(8,128)(2,1)S(1)} custom-call(bf16[128,3584]{1,0:T(8,128)(2,1)S(1)} %get-tuple-element.26.rows_fwd.rows, f32[128,3584]{1,0:T(8,128)S(1)} %get-tuple-element.20.part, bf16[1792,256]{1,0:T(8,128)(2,1)S(1)} %collective-permute-done.4.refs_0_, bf16[1792,256]{1,0:T(8,128)(2,1)S(1)} %collective-permute-done.5.refs_1_, ...), custom_call_target="tpu_custom_call" | custom-call | flops 350000000 | bytes 8000000 | tf_op jit(solution)/shard_map/pallas_call | solution.py:242
  115.5 3.7 %collective-permute-start.11 = (bf16[64,3584]{1,0:T(8,128)(2,1)S(1)}, bf16[64,3584]{1,0:T(8,128)(2,1)S(1)}, u32[]{:S(2)}, u32[]{:S(2)}) collective-permute-start(bf16[64,3584]{1,0:T(8,128)(2,1)S(1)} %slice.47), channel_id=1, source_target_pairs={{0,4},{1,5},{2,6},{3,7},{4,0},{5,1},{6,2},{7,3},{8,12},{9,13},{10,... | collective-permute-start | bytes 1376264 | tf_op jit(solution)/shard_map/ppermute | solution.py:39
  119.2 7.3 %collective-permute-done.12 = bf16[64,3584]{1,0:T(8,128)(2,1)S(1)} collective-permute-done((bf16[64,3584]{1,0:T(8,128)(2,1)S(1)}, bf16[64,3584]{1,0:T(8,128)(2,1)S(1)}, u32[]{:S(2)}, u32[]{:S(2)}) %collective-permute-start.12) | collective-permute-done | bytes 458784 | tf_op jit(solution)/shard_map/ppermute | solution.py:39
  126.6 7.5 %collective-permute-done.11 = bf16[64,3584]{1,0:T(8,128)(2,1)S(1)} collective-permute-done((bf16[64,3584]{1,0:T(8,128)(2,1)S(1)}, bf16[64,3584]{1,0:T(8,128)(2,1)S(1)}, u32[]{:S(2)}, u32[]{:S(2)}) %collective-permute-start.11) | collective-permute-done | bytes 458784 | tf_op jit(solution)/shard_map/ppermute | solution.py:39
  134.4 53.8 %all_to_all.10 = bf16[8,16,3584]{2,1,0:T(8,128)(2,1)S(1)} all-to-all(bf16[8,16,3584]{2,1,0:T(8,128)(2,1)S(1)} %pad_maximum_fusion.1), channel_id=1, replica_groups={{0,8,16,24,32,40,48,56},{1,9,17,25,33,41,49,57},{2,10,18,26,34,42,50,58..., dimensions={0} | all-to-all | bytes 1835008 | tf_op jit(solution)/shard_map/all_to_all | solution.py:44
  (44 shorter events, 17.5 us)
Async XLA Ops:
  0.6 9.1 %collective-permute-start = (bf16[64,3584]{1,0:T(8,128)(2,1)}, bf16[64,3584]{1,0:T(8,128)(2,1)S(1)}, u32[]{:S(2)}, u32[]{:S(2)}) collective-permute-start(bf16[64,3584]{1,0:T(8,128)(2,1)} %bitcast.57), channel_id=1, source_target_pairs={{448,0},{0,64},{64,128},{128,192},{192,256},{256,320},{320,384},{3... | collective-permute-start | bytes 1376264 | tf_op jit(solution)/shard_map/ppermute | solution.py:28
  0.7 9.1 %collective-permute-start.1 = (bf16[64,3584]{1,0:T(8,128)(2,1)}, bf16[64,3584]{1,0:T(8,128)(2,1)S(1)}, u32[]{:S(2)}, u32[]{:S(2)}) collective-permute-start(bf16[64,3584]{1,0:T(8,128)(2,1)} %bitcast.58), channel_id=1, source_target_pairs={{64,0},{128,64},{192,128},{256,192},{320,256},{384,320},{448,384},... | collective-permute-start | bytes 1376264 | tf_op jit(solution)/shard_map/ppermute | solution.py:28
  2.4 45.0 %collective-permute-start.2 = (bf16[3584,256]{1,0:T(8,128)(2,1)}, bf16[3584,256]{1,0:T(8,128)(2,1)S(1)}, u32[]{:S(2)}, u32[]{:S(2)}) collective-permute-start(bf16[3584,256]{1,0:T(8,128)(2,1)} %bitcast.51), channel_id=1, source_target_pairs={{0,1},{1,2},{2,3},{3,0},{4,5},{5,6},{6,7},{7,4},{8,9},{9,10},{10,1... | collective-permute-start | bytes 5505032 | tf_op jit(solution)/shard_map/ppermute | solution.py:34
  4.5 46.3 %collective-permute-start.3 = (bf16[3584,256]{1,0:T(8,128)(2,1)}, bf16[3584,256]{1,0:T(8,128)(2,1)}, u32[]{:S(2)}, u32[]{:S(2)}) collective-permute-start(bf16[3584,256]{1,0:T(8,128)(2,1)} %bitcast.52), channel_id=1, source_target_pairs={{0,3},{1,0},{2,1},{3,2},{4,7},{5,4},{6,5},{7,6},{8,11},{9,8},{10,9... | collective-permute-start | bytes 5505032 | tf_op jit(solution)/shard_map/ppermute | solution.py:34
  9.8 1.6 copy-start.4
  11.4 14.9 %copy-start.6 = (bf16[1,1,512,256]{3,2,1,0:T(8,128)(2,1)S(1)}, bf16[1,1,512,256]{3,2,1,0:T(8,128)(2,1)}, u32[]{:S(2)}) copy-start(bf16[1,1,512,256]{3,2,1,0:T(8,128)(2,1)} %param.17) | copy-start | bytes 786436
  11.4 64.1 %all-to-all-start = ((bf16[8,16,3584]{2,1,0:T(8,128)(2,1)}), bf16[8,16,3584]{2,1,0:T(8,128)(2,1)}, u32[]{:S(2)}, u32[]{:S(2)}) async-start(bf16[8,16,3584]{2,1,0:T(8,128)(2,1)} %bitcast.4), calls=%async_computation | async-start | bytes 1835008 | tf_op jit(solution)/shard_map/all_to_all | solution.py:44
  30.0 47.4 %collective-permute-start.7 = (bf16[2176,256]{1,0:T(8,128)(2,1)}, bf16[2176,256]{1,0:T(8,128)(2,1)S(1)}, u32[]{:S(2)}, u32[]{:S(2)}) collective-permute-start(bf16[2176,256]{1,0:T(8,128)(2,1)} %shard_map.124), channel_id=1, source_target_pairs={{0,1},{1,2},{2,3},{3,0},{4,5},{5,6},{6,7},{7,4},{8,9},{9,10},{10,1... | collective-permute-start | bytes 3342344 | tf_op jit(solution)/shard_map/ppermute | solution.py:34
  33.4 46.2 %collective-permute-start.8 = (bf16[2176,256]{1,0:T(8,128)(2,1)}, bf16[2176,256]{1,0:T(8,128)(2,1)}, u32[]{:S(2)}, u32[]{:S(2)}) collective-permute-start(bf16[2176,256]{1,0:T(8,128)(2,1)} %shard_map.124), channel_id=1, source_target_pairs={{0,3},{1,0},{2,1},{3,2},{4,7},{5,4},{6,5},{7,6},{8,11},{9,8},{10,9... | collective-permute-start | bytes 3342344 | tf_op jit(solution)/shard_map/ppermute | solution.py:34
  47.4 3.5 %copy-start.2 = (bf16[3584,256]{1,0:T(8,128)(2,1)}, bf16[3584,256]{1,0:T(8,128)(2,1)S(1)}, u32[]{:S(2)}) copy-start(bf16[3584,256]{1,0:T(8,128)(2,1)S(1)} %collective-permute-done.2.behind.refs_2_) | copy-start | bytes 5505028
  53.7 37.2 %collective-permute-start.4 = (bf16[1792,256]{1,0:T(8,128)(2,1)}, bf16[1792,256]{1,0:T(8,128)(2,1)S(1)}, u32[]{:S(2)}, u32[]{:S(2)}) collective-permute-start(bf16[1792,256]{1,0:T(8,128)(2,1)} %get-tuple-element.16), channel_id=1, source_target_pairs={{0,1},{1,2},{2,3},{3,0},{4,5},{5,6},{6,7},{7,4},{8,9},{9,10},{10,1... | collective-permute-start | bytes 2752520 | tf_op jit(solution)/shard_map/ppermute | solution.py:34
  56.0 38.3 %collective-permute-start.5 = (bf16[1792,256]{1,0:T(8,128)(2,1)}, bf16[1792,256]{1,0:T(8,128)(2,1)S(1)}, u32[]{:S(2)}, u32[]{:S(2)}) collective-permute-start(bf16[1792,256]{1,0:T(8,128)(2,1)} %get-tuple-element.17), channel_id=1, source_target_pairs={{0,3},{1,0},{2,1},{3,2},{4,7},{5,4},{6,5},{7,6},{8,11},{9,8},{10,9... | collective-permute-start | bytes 2752520 | tf_op jit(solution)/shard_map/ppermute | solution.py:34
  75.5 24.1 %collective-permute-start.6 = (bf16[8,16,3584]{2,1,0:T(8,128)(2,1)}, bf16[8,16,3584]{2,1,0:T(8,128)(2,1)S(1)}, u32[]{:S(2)}, u32[]{:S(2)}) collective-permute-start(bf16[8,16,3584]{2,1,0:T(8,128)(2,1)} %all-to-all-done), channel_id=1, source_target_pairs={{0,4},{1,5},{2,6},{3,7},{4,0},{5,1},{6,2},{7,3},{8,12},{9,13},{10,... | collective-permute-start | bytes 2752520 | tf_op jit(solution)/shard_map/ppermute | solution.py:39
  77.5 31.3 %collective-permute-start.9 = (bf16[1024,256]{1,0:T(8,128)(2,1)S(1)}, bf16[1024,256]{1,0:T(8,128)(2,1)S(1)}, u32[]{:S(2)}, u32[]{:S(2)}) collective-permute-start(bf16[1024,256]{1,0:T(8,128)(2,1)S(1)} %slice.44), channel_id=1, source_target_pairs={{0,1},{1,2},{2,3},{3,0},{4,5},{5,6},{6,7},{7,4},{8,9},{9,10},{10,1... | collective-permute-start | bytes 1572872 | tf_op jit(solution)/shard_map/ppermute | solution.py:34
  80.6 28.2 %collective-permute-start.10 = (bf16[896,256]{1,0:T(8,128)(2,1)S(1)}, bf16[896,256]{1,0:T(8,128)(2,1)S(1)}, u32[]{:S(2)}, u32[]{:S(2)}) collective-permute-start(bf16[896,256]{1,0:T(8,128)(2,1)S(1)} %slice.45), channel_id=1, source_target_pairs={{0,3},{1,0},{2,1},{3,2},{4,7},{5,4},{6,5},{7,6},{8,11},{9,8},{10,9... | collective-permute-start | bytes 1376264 | tf_op jit(solution)/shard_map/ppermute | solution.py:34
  100.9 1.5 copy-start.3
  101.1 1.6 copy-start
  101.1 2.2 %copy-start.1 = (bf16[1,1,3584,256]{3,2,1,0:T(8,128)(2,1)S(1)}, bf16[1,1,3584,256]{3,2,1,0:T(8,128)(2,1)}, u32[]{:S(2)}) copy-start(bf16[1,1,3584,256]{3,2,1,0:T(8,128)(2,1)} %param.15) | copy-start | bytes 5505028
  111.2 15.3 %collective-permute-start.12 = (bf16[64,3584]{1,0:T(8,128)(2,1)S(1)}, bf16[64,3584]{1,0:T(8,128)(2,1)S(1)}, u32[]{:S(2)}, u32[]{:S(2)}) collective-permute-start(bf16[64,3584]{1,0:T(8,128)(2,1)S(1)} %slice.49), channel_id=1, source_target_pairs={{0,4},{1,5},{2,6},{3,7},{4,0},{5,1},{6,2},{7,3},{8,12},{9,13},{10,... | collective-permute-start | bytes 1376264 | tf_op jit(solution)/shard_map/ppermute | solution.py:39
  115.5 18.6 %collective-permute-start.11 = (bf16[64,3584]{1,0:T(8,128)(2,1)S(1)}, bf16[64,3584]{1,0:T(8,128)(2,1)S(1)}, u32[]{:S(2)}, u32[]{:S(2)}) collective-permute-start(bf16[64,3584]{1,0:T(8,128)(2,1)S(1)} %slice.47), channel_id=1, source_target_pairs={{0,4},{1,5},{2,6},{3,7},{4,0},{5,1},{6,2},{7,3},{8,12},{9,13},{10,... | collective-permute-start | bytes 1376264 | tf_op jit(solution)/shard_map/ppermute | solution.py:39
  134.3 53.8 %copy-start.5 = (bf16[64,3584]{1,0:T(8,128)(2,1)S(1)}, bf16[64,3584]{1,0:T(8,128)(2,1)}, u32[]{:S(2)}) copy-start(bf16[64,3584]{1,0:T(8,128)(2,1)} %copy-done.4) | copy-start | bytes 1376260

commit v3 on v2

--- a/solution.py
+++ b/solution.py
@@ -16,7 +16,7 @@
 PART = 8
 ACROSS = 1792
 NEXT = ACROSS + 128
-TOTAL = NEXT + 256
+TOTAL = NEXT + 128
 CHUNKS = ((0, 896), (896, 896), (FIRST, 896), (FIRST + 896, 896))
 WIDTH = 256
 HIDDEN = 128
@@ -89,19 +89,14 @@
     backward_out[...] = (back_wide + grad_start).astype(backward_out.dtype)
 
 
-def gather_kernel(down_own, saved_across, saved_next, saved_previous, held, sems):
-    pieces = [
-        (saved_across, held.at[pl.ds(ACROSS, 128)]),
-        (saved_next, held.at[pl.ds(NEXT, 128)]),
-        (saved_previous, held.at[pl.ds(NEXT + 128, 128)]),
-    ]
-    for c in range(down_own.shape[1] // WIDTH):
-        pieces.append(
-            (
-                down_own.at[:, pl.ds(c * WIDTH, WIDTH)],
-                held.at[pl.ds(c * HIDDEN, HIDDEN)],
-            )
-        )
+def gather_kernel(down_own, saved_across, saved_next, saved_previous, held_next, held_previous, sems):
+    pieces = []
+    for held, saved in ((held_next, saved_next), (held_previous, saved_previous)):
+        pieces.append((saved_across, held.at[pl.ds(ACROSS, 128)]))
+        pieces.append((saved, held.at[pl.ds(NEXT, 128)]))
+        for c in range(down_own.shape[1] // WIDTH):
+            block = down_own.at[:, pl.ds(c * WIDTH, WIDTH)]
+            pieces.append((block, held.at[pl.ds(c * HIDDEN, HIDDEN)]))
     copies = [pltpu.make_async_copy(p[0], p[1], sems.at[i]) for i, p in enumerate(pieces)]
     for copy in copies:
         copy.start()
@@ -192,15 +187,9 @@
 
 
 def forward_kernel(rows, part, *refs):
-    sources, out, buffers, sems = refs[:4], refs[4], refs[5:9], refs[9]
-    copies = fetch(sources, buffers, sems)
-    first, last, down_first, down_last = buffers
-    copies[0].wait()
+    first, last, down_first, down_last, out = refs
     pre = mm(rows[:, :FIRST], first[...])
-    copies[1].wait()
     act = activate(pre + mm(rows[:, FIRST:], last[...]))
-    copies[2].wait()
-    copies[3].wait()
     count = rows.shape[1] // WIDTH
     blocks = down_blocks(down_first, 0, PART) + down_blocks(down_last, 0, count - PART)
     for c, block in enumerate(blocks):
@@ -209,17 +198,11 @@
 
 
 def backward_kernel(rows, part, *refs):
-    sources, out, buffers, sems = refs[:4], refs[4], refs[5:9], refs[9]
-    copies = fetch(sources, buffers, sems)
-    first, last, down_first, down_last = buffers
-    copies[2].wait()
-    copies[3].wait()
+    first, last, down_first, down_last, out = refs
     middle = PART * WIDTH
     grad_act = across_blocks(rows[:, :middle], down_first, 0)
     grad_act += across_blocks(rows[:, middle:], down_last, 0)
     grad = slope(grad_act, *factors(down_last[ACROSS - PART * HIDDEN :]))
-    copies[0].wait()
-    copies[1].wait()
     for start, size in CHUNKS:
         columns = slice(start, start + size)
         weights = first[columns] if start < FIRST else last[start - FIRST : start - FIRST + size]
@@ -278,16 +261,16 @@
         return jnp.concatenate([mine, other]).reshape(-1, WIDTH)
 
     left = pl.BlockSpec(memory_space=pl.ANY)
-    held = pl.pallas_call(
+    held_next, held_previous = pl.pallas_call(
         gather_kernel,
-        out_shape=jax.ShapeDtypeStruct((TOTAL, WIDTH), in_own.dtype),
+        out_shape=[jax.ShapeDtypeStruct((TOTAL, WIDTH), in_own.dtype)] * 2,
         in_specs=[left] * 4,
-        out_specs=pl.BlockSpec(memory_space=pltpu.VMEM),
-        scratch_shapes=[pltpu.SemaphoreType.DMA((3 + features // WIDTH,))],
+        out_specs=[pl.BlockSpec(memory_space=pltpu.VMEM)] * 2,
+        scratch_shapes=[pltpu.SemaphoreType.DMA((4 + 2 * (features // WIDTH),))],
         cost_estimate=pl.CostEstimate(flops=0, bytes_accessed=2_000_000, transcendentals=0),
     )(down_own, saved_for(2), saved_for(1), saved_for(-1))
     behind_in, ahead_in = shift_y(in_own, 1), shift_y(in_own, -1)
-    behind, ahead = shift_y(held, 1), shift_y(held, -1)
+    behind, ahead = shift_y(held_next, 1), shift_y(held_previous, -1)
 
     routes = [route.reshape(1, BLOCK).astype(jnp.float32) for route in (route_fwd, route_bwd)]
     values = jnp.concatenate(
@@ -314,12 +297,12 @@
     far_in = (shift_y(halves[0], 1), shift_y(halves[1], -1))
     partner = swap_z(own)
     far_in, partner, saved_behind = lax.optimization_barrier(
-        (far_in, partner, behind[NEXT : NEXT + 128])
+        (far_in, partner, behind[NEXT:])
     )
     (factor,) = call(
         factor_kernel,
         [((384, WIDTH), jnp.float32)],
-        (saved_for(0), saved_behind, ahead[NEXT + 128 :]),
+        (saved_for(0), saved_behind, ahead[NEXT:]),
         flops=1_000_000_000,
     )
     far_down = (
@@ -339,9 +322,9 @@
         flops=2_000_000_000,
         traffic=0,
     )
-    (part,) = call(forward_kernel, [(narrow, jnp.bfloat16)], (rows_fwd, part), far, 350_000_000)
+    (part,) = call(forward_kernel, [(narrow, jnp.bfloat16)], (rows_fwd, part, *far), flops=350_000_000)
     received_fwd = swap_z(part[BLOCK:])
-    (grad_part,) = call(backward_kernel, [(narrow, jnp.bfloat16)], (rows_bwd, grad_part), far, 350_000_000)
+    (grad_part,) = call(backward_kernel, [(narrow, jnp.bfloat16)], (rows_bwd, grad_part, *far), flops=350_000_000)
     received_bwd = swap_z(grad_part[BLOCK:])
 
     def add(product, received):

time: 190 us -> 188 us (0.989)
    ppermute x3, waiting for transfers between devices: 20.1 us -> 22.5 us  [swap_z(): return lax.ppermute(block, 'expert', [(k, k ^ ROWS) for k in range(size)])]
    ppermute x8, waiting for transfers between devices: 24 us -> 21.7 us  [shift_y(): return lax.ppermute(block, 'expert', route)]
where the time goes in v3:
time: 188 us; the launch traced here: 187 us
  waiting for transfers between devices  60.3 us (32%)
  blocking collectives  52.5 us (28%)
  starting transfers between devices  47.7 us (25%)
  Pallas kernels  17 us (9%)
  local copies, waits for them, and re-layouts  5.12 us (3%)
  other arithmetic  3.6 us (2%)
    all_to_all x1, blocking collectives, exchange_z(): lax.all_to_all(block, 'expert', split_axis=0, concat_axis=0, axis_index_g...  52.5 us
    ppermute x8, starting transfers between devices, shift_y(): return lax.ppermute(block, 'expert', route)  23.4 us
    ppermute x3, waiting for transfers between devices, swap_z(): return lax.ppermute(block, 'expert', [(k, k ^ ROWS) for k in range(size)])  22.5 us
    ppermute x8, waiting for transfers between devices, shift_y(): return lax.ppermute(block, 'expert', route)  21.7 us
    all_to_all x1, waiting for transfers between devices, exchange_z(): lax.all_to_all(block, 'expert', split_axis=0, concat_axis=0, axis_index_g...  16.1 us
    all_to_all x1, starting transfers between devices, exchange_z(): lax.all_to_all(block, 'expert', split_axis=0, concat_axis=0, axis_index_g...  14.9 us
    pallas_call x6, Pallas kernels, call(): pl.pallas_call(kernel, out_shape=[jax.ShapeDtypeStruct(shape, dtype) for...  11.1 us
    ppermute x3, starting transfers between devices, swap_z(): return lax.ppermute(block, 'expert', [(k, k ^ ROWS) for k in range(size)])  7.75 us
  transfers between devices with their start and end apart: 14, of which 8 were waited for; matrix products, arithmetic and copies ran while one was open for 3% of the time, Pallas kernels for 8%

profile of v3, /device:TPU:90, one launch (start us, length us, event | category | flops | bytes accessed | tf_op | source)
XLA Modules:
  0.0 187.3 jit_solution(14346138359540696811)
XLA Ops:
  2.4 2.1 %collective-permute-start.2 = (bf16[3584,256]{1,0:T(8,128)(2,1)}, bf16[3584,256]{1,0:T(8,128)(2,1)S(1)}, u32[]{:S(2)}, u32[]{:S(2)}) collective-permute-start(bf16[3584,256]{1,0:T(8,128)(2,1)} %bitcast.51), channel_id=1, source_target_pairs={{0,1},{1,2},{2,3},{3,0},{4,5},{5,6},{6,7},{7,4},{8,9},{9,10},{10,1... | collective-permute-start | bytes 5505032 | tf_op jit(solution)/shard_map/ppermute | solution.py:34
  4.5 3.7 %collective-permute-start.3 = (bf16[3584,256]{1,0:T(8,128)(2,1)}, bf16[3584,256]{1,0:T(8,128)(2,1)}, u32[]{:S(2)}, u32[]{:S(2)}) collective-permute-start(bf16[3584,256]{1,0:T(8,128)(2,1)} %bitcast.52), channel_id=1, source_target_pairs={{0,3},{1,0},{2,1},{3,2},{4,7},{5,4},{6,5},{7,6},{8,11},{9,8},{10,9... | collective-permute-start | bytes 5505032 | tf_op jit(solution)/shard_map/ppermute | solution.py:34
  11.4 14.9 %all-to-all-start = ((bf16[8,16,3584]{2,1,0:T(8,128)(2,1)}), bf16[8,16,3584]{2,1,0:T(8,128)(2,1)}, u32[]{:S(2)}, u32[]{:S(2)}) async-start(bf16[8,16,3584]{2,1,0:T(8,128)(2,1)} %bitcast.4), calls=%async_computation | async-start | bytes 1835008 | tf_op jit(solution)/shard_map/all_to_all | solution.py:44
  27.6 3.3 %shard_map.124 = (bf16[2048,256]{1,0:T(8,128)(2,1)}, bf16[2048,256]{1,0:T(8,128)(2,1)}) custom-call(bf16[128,3584]{1,0:T(8,128)(2,1)} %bitcast.49, bf16[128,256]{1,0:T(8,128)(2,1)} %get-tuple-element.42.saved_across, bf16[128,256]{1,0:T(8,128)(2,1)} %get-tuple-element.43.saved_next, bf16[128,256]{1,0:T(8,128)(2,1)} %maximum_bitcast_fusion.2.saved_previous), custom_call_target="tpu_custom_call" | custom-call | bytes 2000000 | tf_op jit(solution)/shard_map/pallas_call | solution.py:264
  30.9 3.3 %collective-permute-start.7 = (bf16[2048,256]{1,0:T(8,128)(2,1)}, bf16[2048,256]{1,0:T(8,128)(2,1)S(1)}, u32[]{:S(2)}, u32[]{:S(2)}) collective-permute-start(bf16[2048,256]{1,0:T(8,128)(2,1)} %get-tuple-element.20), channel_id=1, source_target_pairs={{0,1},{1,2},{2,3},{3,0},{4,5},{5,6},{6,7},{7,4},{8,9},{9,10},{10,1... | collective-permute-start | bytes 3145736 | tf_op jit(solution)/shard_map/ppermute | solution.py:34
  34.2 2.5 %collective-permute-start.8 = (bf16[2048,256]{1,0:T(8,128)(2,1)}, bf16[2048,256]{1,0:T(8,128)(2,1)}, u32[]{:S(2)}, u32[]{:S(2)}) collective-permute-start(bf16[2048,256]{1,0:T(8,128)(2,1)} %get-tuple-element.23), channel_id=1, source_target_pairs={{0,3},{1,0},{2,1},{3,2},{4,7},{5,4},{6,5},{7,6},{8,11},{9,8},{10,9... | collective-permute-start | bytes 3145736 | tf_op jit(solution)/shard_map/ppermute | solution.py:34
  36.8 10.6 %collective-permute-done.2.behind.refs_2_ = bf16[3584,256]{1,0:T(8,128)(2,1)S(1)} collective-permute-done((bf16[3584,256]{1,0:T(8,128)(2,1)}, bf16[3584,256]{1,0:T(8,128)(2,1)S(1)}, u32[]{:S(2)}, u32[]{:S(2)}) %collective-permute-start.2) | collective-permute-done | bytes 1835040 | tf_op jit(solution)/shard_map/ppermute | solution.py:34
  47.4 3.5 %collective-permute-done.3.ahead.refs_4_ = bf16[3584,256]{1,0:T(8,128)(2,1)} collective-permute-done((bf16[3584,256]{1,0:T(8,128)(2,1)}, bf16[3584,256]{1,0:T(8,128)(2,1)}, u32[]{:S(2)}, u32[]{:S(2)}) %collective-permute-start.3) | collective-permute-done | bytes 1835040 | tf_op jit(solution)/shard_map/ppermute | solution.py:34
  50.9 2.7 %shard_map.123 = (bf16[1792,256]{1,0:T(8,128)(2,1)}, bf16[1792,256]{1,0:T(8,128)(2,1)}) custom-call(bf16[3584,256]{1,0:T(8,128)(2,1)} %copy-done.2, bf16[3584,256]{1,0:T(8,128)(2,1)} %collective-permute-done.3.ahead.refs_4_), custom_call_target="tpu_custom_call" | custom-call | flops 20000000000 | bytes 4000000 | tf_op jit(solution)/shard_map/pallas_call | solution.py:289
  53.6 2.3 %collective-permute-start.4 = (bf16[1792,256]{1,0:T(8,128)(2,1)}, bf16[1792,256]{1,0:T(8,128)(2,1)S(1)}, u32[]{:S(2)}, u32[]{:S(2)}) collective-permute-start(bf16[1792,256]{1,0:T(8,128)(2,1)} %get-tuple-element.18), channel_id=1, source_target_pairs={{0,1},{1,2},{2,3},{3,0},{4,5},{5,6},{6,7},{7,4},{8,9},{9,10},{10,1... | collective-permute-start | bytes 2752520 | tf_op jit(solution)/shard_map/ppermute | solution.py:34
  55.9 3.6 %collective-permute-start.5 = (bf16[1792,256]{1,0:T(8,128)(2,1)}, bf16[1792,256]{1,0:T(8,128)(2,1)S(1)}, u32[]{:S(2)}, u32[]{:S(2)}) collective-permute-start(bf16[1792,256]{1,0:T(8,128)(2,1)} %get-tuple-element.19), channel_id=1, source_target_pairs={{0,3},{1,0},{2,1},{3,2},{4,7},{5,4},{6,5},{7,6},{8,11},{9,8},{10,9... | collective-permute-start | bytes 2752520 | tf_op jit(solution)/shard_map/ppermute | solution.py:34
  59.5 16.1 %all-to-all-done = bf16[8,16,3584]{2,1,0:T(8,128)(2,1)} async-done(((bf16[8,16,3584]{2,1,0:T(8,128)(2,1)}), bf16[8,16,3584]{2,1,0:T(8,128)(2,1)}, u32[]{:S(2)}, u32[]{:S(2)}) %all-to-all-start) | async-done | bytes 917536 | tf_op jit(solution)/shard_map/all_to_all | solution.py:44
  75.5 1.9 %collective-permute-start.6 = (bf16[8,16,3584]{2,1,0:T(8,128)(2,1)}, bf16[8,16,3584]{2,1,0:T(8,128)(2,1)S(1)}, u32[]{:S(2)}, u32[]{:S(2)}) collective-permute-start(bf16[8,16,3584]{2,1,0:T(8,128)(2,1)} %all-to-all-done), channel_id=1, source_target_pairs={{0,4},{1,5},{2,6},{3,7},{4,0},{5,1},{6,2},{7,3},{8,12},{9,13},{10,... | collective-permute-start | bytes 2752520 | tf_op jit(solution)/shard_map/ppermute | solution.py:39
  77.5 2.1 %collective-permute-start.9 = (bf16[1024,256]{1,0:T(8,128)(2,1)S(1)}, bf16[1024,256]{1,0:T(8,128)(2,1)S(1)}, u32[]{:S(2)}, u32[]{:S(2)}) collective-permute-start(bf16[1024,256]{1,0:T(8,128)(2,1)S(1)} %slice.44), channel_id=1, source_target_pairs={{0,1},{1,2},{2,3},{3,0},{4,5},{5,6},{6,7},{7,4},{8,9},{9,10},{10,1... | collective-permute-start | bytes 1572872 | tf_op jit(solution)/shard_map/ppermute | solution.py:34
  80.7 3.7 %collective-permute-start.10 = (bf16[896,256]{1,0:T(8,128)(2,1)S(1)}, bf16[896,256]{1,0:T(8,128)(2,1)S(1)}, u32[]{:S(2)}, u32[]{:S(2)}) collective-permute-start(bf16[896,256]{1,0:T(8,128)(2,1)S(1)} %slice.45), channel_id=1, source_target_pairs={{0,3},{1,0},{2,1},{3,2},{4,7},{5,4},{6,5},{7,6},{8,11},{9,8},{10,9... | collective-permute-start | bytes 1376264 | tf_op jit(solution)/shard_map/ppermute | solution.py:34
  85.3 4.2 %collective-permute-done.4.refs_0_ = bf16[1792,256]{1,0:T(8,128)(2,1)S(1)} collective-permute-done((bf16[1792,256]{1,0:T(8,128)(2,1)}, bf16[1792,256]{1,0:T(8,128)(2,1)S(1)}, u32[]{:S(2)}, u32[]{:S(2)}) %collective-permute-start.4) | collective-permute-done | bytes 917536 | tf_op jit(solution)/shard_map/ppermute | solution.py:34
  89.5 3.4 %collective-permute-done.5.refs_1_ = bf16[1792,256]{1,0:T(8,128)(2,1)S(1)} collective-permute-done((bf16[1792,256]{1,0:T(8,128)(2,1)}, bf16[1792,256]{1,0:T(8,128)(2,1)S(1)}, u32[]{:S(2)}, u32[]{:S(2)}) %collective-permute-start.5) | collective-permute-done | bytes 917536 | tf_op jit(solution)/shard_map/ppermute | solution.py:34
  92.9 6.7 %collective-permute-done.6 = bf16[8,16,3584]{2,1,0:T(8,128)(2,1)S(1)} collective-permute-done((bf16[8,16,3584]{2,1,0:T(8,128)(2,1)}, bf16[8,16,3584]{2,1,0:T(8,128)(2,1)S(1)}, u32[]{:S(2)}, u32[]{:S(2)}) %collective-permute-start.6) | collective-permute-done | bytes 917536 | tf_op jit(solution)/shard_map/ppermute | solution.py:39
  103.3 5.4 %shard_map.126 = (f32[128,3584]{1,0:T(8,128)S(1)}, f32[128,3584]{1,0:T(8,128)S(1)}) custom-call(bf16[128,3584]{1,0:T(8,128)(2,1)S(1)} %get-tuple-element.30.rows_fwd.rows, bf16[128,3584]{1,0:T(8,128)(2,1)S(1)} %get-tuple-element.31.rows_bwd.rows, f32[384,256]{1,0:T(8,128)S(1)} %shard_map.125.factor, bf16[3584,256]{1,0:T(8,128)(2,1)S(1)} %bitcast.53, ...), custom_call_target="tpu_custom_call" | custom-call | flops 2000000000 | tf_op jit(solution)/shard_map/pallas_call | solution.py:225
  110.2 2.2 %collective-permute-start.12 = (bf16[64,3584]{1,0:T(8,128)(2,1)S(1)}, bf16[64,3584]{1,0:T(8,128)(2,1)S(1)}, u32[]{:S(2)}, u32[]{:S(2)}) collective-permute-start(bf16[64,3584]{1,0:T(8,128)(2,1)S(1)} %slice.49), channel_id=1, source_target_pairs={{0,4},{1,5},{2,6},{3,7},{4,0},{5,1},{6,2},{7,3},{8,12},{9,13},{10,... | collective-permute-start | bytes 1376264 | tf_op jit(solution)/shard_map/ppermute | solution.py:39
  113.7 3.6 %collective-permute-start.11 = (bf16[64,3584]{1,0:T(8,128)(2,1)S(1)}, bf16[64,3584]{1,0:T(8,128)(2,1)S(1)}, u32[]{:S(2)}, u32[]{:S(2)}) collective-permute-start(bf16[64,3584]{1,0:T(8,128)(2,1)S(1)} %slice.47), channel_id=1, source_target_pairs={{0,4},{1,5},{2,6},{3,7},{4,0},{5,1},{6,2},{7,3},{8,12},{9,13},{10,... | collective-permute-start | bytes 1376264 | tf_op jit(solution)/shard_map/ppermute | solution.py:39
  117.3 8.2 %collective-permute-done.12 = bf16[64,3584]{1,0:T(8,128)(2,1)S(1)} collective-permute-done((bf16[64,3584]{1,0:T(8,128)(2,1)S(1)}, bf16[64,3584]{1,0:T(8,128)(2,1)S(1)}, u32[]{:S(2)}, u32[]{:S(2)}) %collective-permute-start.12) | collective-permute-done | bytes 458784 | tf_op jit(solution)/shard_map/ppermute | solution.py:39
  125.7 7.5 %collective-permute-done.11 = bf16[64,3584]{1,0:T(8,128)(2,1)S(1)} collective-permute-done((bf16[64,3584]{1,0:T(8,128)(2,1)S(1)}, bf16[64,3584]{1,0:T(8,128)(2,1)S(1)}, u32[]{:S(2)}, u32[]{:S(2)}) %collective-permute-start.11) | collective-permute-done | bytes 458784 | tf_op jit(solution)/shard_map/ppermute | solution.py:39
  133.4 52.5 %all_to_all.10 = bf16[8,16,3584]{2,1,0:T(8,128)(2,1)S(1)} all-to-all(bf16[8,16,3584]{2,1,0:T(8,128)(2,1)S(1)} %pad_maximum_fusion.1), channel_id=1, replica_groups={{0,8,16,24,32,40,48,56},{1,9,17,25,33,41,49,57},{2,10,18,26,34,42,50,58..., dimensions={0} | all-to-all | bytes 1835008 | tf_op jit(solution)/shard_map/all_to_all | solution.py:44
  (44 shorter events, 16.2 us)
Async XLA Ops:
  0.6 9.1 %collective-permute-start = (bf16[64,3584]{1,0:T(8,128)(2,1)}, bf16[64,3584]{1,0:T(8,128)(2,1)S(1)}, u32[]{:S(2)}, u32[]{:S(2)}) collective-permute-start(bf16[64,3584]{1,0:T(8,128)(2,1)} %bitcast.57), channel_id=1, source_target_pairs={{448,0},{0,64},{64,128},{128,192},{192,256},{256,320},{320,384},{3... | collective-permute-start | bytes 1376264 | tf_op jit(solution)/shard_map/ppermute | solution.py:28
  0.7 9.1 %collective-permute-start.1 = (bf16[64,3584]{1,0:T(8,128)(2,1)}, bf16[64,3584]{1,0:T(8,128)(2,1)S(1)}, u32[]{:S(2)}, u32[]{:S(2)}) collective-permute-start(bf16[64,3584]{1,0:T(8,128)(2,1)} %bitcast.58), channel_id=1, source_target_pairs={{64,0},{128,64},{192,128},{256,192},{320,256},{384,320},{448,384},... | collective-permute-start | bytes 1376264 | tf_op jit(solution)/shard_map/ppermute | solution.py:28
  2.4 45.0 %collective-permute-start.2 = (bf16[3584,256]{1,0:T(8,128)(2,1)}, bf16[3584,256]{1,0:T(8,128)(2,1)S(1)}, u32[]{:S(2)}, u32[]{:S(2)}) collective-permute-start(bf16[3584,256]{1,0:T(8,128)(2,1)} %bitcast.51), channel_id=1, source_target_pairs={{0,1},{1,2},{2,3},{3,0},{4,5},{5,6},{6,7},{7,4},{8,9},{9,10},{10,1... | collective-permute-start | bytes 5505032 | tf_op jit(solution)/shard_map/ppermute | solution.py:34
  4.5 46.3 %collective-permute-start.3 = (bf16[3584,256]{1,0:T(8,128)(2,1)}, bf16[3584,256]{1,0:T(8,128)(2,1)}, u32[]{:S(2)}, u32[]{:S(2)}) collective-permute-start(bf16[3584,256]{1,0:T(8,128)(2,1)} %bitcast.52), channel_id=1, source_target_pairs={{0,3},{1,0},{2,1},{3,2},{4,7},{5,4},{6,5},{7,6},{8,11},{9,8},{10,9... | collective-permute-start | bytes 5505032 | tf_op jit(solution)/shard_map/ppermute | solution.py:34
  9.8 1.7 copy-start.4
  11.4 14.9 %copy-start.6 = (bf16[1,1,512,256]{3,2,1,0:T(8,128)(2,1)S(1)}, bf16[1,1,512,256]{3,2,1,0:T(8,128)(2,1)}, u32[]{:S(2)}) copy-start(bf16[1,1,512,256]{3,2,1,0:T(8,128)(2,1)} %param.17) | copy-start | bytes 786436
  11.4 64.1 %all-to-all-start = ((bf16[8,16,3584]{2,1,0:T(8,128)(2,1)}), bf16[8,16,3584]{2,1,0:T(8,128)(2,1)}, u32[]{:S(2)}, u32[]{:S(2)}) async-start(bf16[8,16,3584]{2,1,0:T(8,128)(2,1)} %bitcast.4), calls=%async_computation | async-start | bytes 1835008 | tf_op jit(solution)/shard_map/all_to_all | solution.py:44
  30.9 46.6 %collective-permute-start.7 = (bf16[2048,256]{1,0:T(8,128)(2,1)}, bf16[2048,256]{1,0:T(8,128)(2,1)S(1)}, u32[]{:S(2)}, u32[]{:S(2)}) collective-permute-start(bf16[2048,256]{1,0:T(8,128)(2,1)} %get-tuple-element.20), channel_id=1, source_target_pairs={{0,1},{1,2},{2,3},{3,0},{4,5},{5,6},{6,7},{7,4},{8,9},{9,10},{10,1... | collective-permute-start | bytes 3145736 | tf_op jit(solution)/shard_map/ppermute | solution.py:34
  34.2 45.4 %collective-permute-start.8 = (bf16[2048,256]{1,0:T(8,128)(2,1)}, bf16[2048,256]{1,0:T(8,128)(2,1)}, u32[]{:S(2)}, u32[]{:S(2)}) collective-permute-start(bf16[2048,256]{1,0:T(8,128)(2,1)} %get-tuple-element.23), channel_id=1, source_target_pairs={{0,3},{1,0},{2,1},{3,2},{4,7},{5,4},{6,5},{7,6},{8,11},{9,8},{10,9... | collective-permute-start | bytes 3145736 | tf_op jit(solution)/shard_map/ppermute | solution.py:34
  47.4 3.5 %copy-start.2 = (bf16[3584,256]{1,0:T(8,128)(2,1)}, bf16[3584,256]{1,0:T(8,128)(2,1)S(1)}, u32[]{:S(2)}) copy-start(bf16[3584,256]{1,0:T(8,128)(2,1)S(1)} %collective-permute-done.2.behind.refs_2_) | copy-start | bytes 5505028
  53.6 35.9 %collective-permute-start.4 = (bf16[1792,256]{1,0:T(8,128)(2,1)}, bf16[1792,256]{1,0:T(8,128)(2,1)S(1)}, u32[]{:S(2)}, u32[]{:S(2)}) collective-permute-start(bf16[1792,256]{1,0:T(8,128)(2,1)} %get-tuple-element.18), channel_id=1, source_target_pairs={{0,1},{1,2},{2,3},{3,0},{4,5},{5,6},{6,7},{7,4},{8,9},{9,10},{10,1... | collective-permute-start | bytes 2752520 | tf_op jit(solution)/shard_map/ppermute | solution.py:34
  55.9 37.0 %collective-permute-start.5 = (bf16[1792,256]{1,0:T(8,128)(2,1)}, bf16[1792,256]{1,0:T(8,128)(2,1)S(1)}, u32[]{:S(2)}, u32[]{:S(2)}) collective-permute-start(bf16[1792,256]{1,0:T(8,128)(2,1)} %get-tuple-element.19), channel_id=1, source_target_pairs={{0,3},{1,0},{2,1},{3,2},{4,7},{5,4},{6,5},{7,6},{8,11},{9,8},{10,9... | collective-permute-start | bytes 2752520 | tf_op jit(solution)/shard_map/ppermute | solution.py:34
  75.5 24.1 %collective-permute-start.6 = (bf16[8,16,3584]{2,1,0:T(8,128)(2,1)}, bf16[8,16,3584]{2,1,0:T(8,128)(2,1)S(1)}, u32[]{:S(2)}, u32[]{:S(2)}) collective-permute-start(bf16[8,16,3584]{2,1,0:T(8,128)(2,1)} %all-to-all-done), channel_id=1, source_target_pairs={{0,4},{1,5},{2,6},{3,7},{4,0},{5,1},{6,2},{7,3},{8,12},{9,13},{10,... | collective-permute-start | bytes 2752520 | tf_op jit(solution)/shard_map/ppermute | solution.py:39
  77.5 31.2 %collective-permute-start.9 = (bf16[1024,256]{1,0:T(8,128)(2,1)S(1)}, bf16[1024,256]{1,0:T(8,128)(2,1)S(1)}, u32[]{:S(2)}, u32[]{:S(2)}) collective-permute-start(bf16[1024,256]{1,0:T(8,128)(2,1)S(1)} %slice.44), channel_id=1, source_target_pairs={{0,1},{1,2},{2,3},{3,0},{4,5},{5,6},{6,7},{7,4},{8,9},{9,10},{10,1... | collective-permute-start | bytes 1572872 | tf_op jit(solution)/shard_map/ppermute | solution.py:34
  80.7 28.0 %collective-permute-start.10 = (bf16[896,256]{1,0:T(8,128)(2,1)S(1)}, bf16[896,256]{1,0:T(8,128)(2,1)S(1)}, u32[]{:S(2)}, u32[]{:S(2)}) collective-permute-start(bf16[896,256]{1,0:T(8,128)(2,1)S(1)} %slice.45), channel_id=1, source_target_pairs={{0,3},{1,0},{2,1},{3,2},{4,7},{5,4},{6,5},{7,6},{8,11},{9,8},{10,9... | collective-permute-start | bytes 1376264 | tf_op jit(solution)/shard_map/ppermute | solution.py:34
  101.0 1.5 copy-start.3
  101.1 1.6 copy-start
  101.1 2.2 %copy-start.1 = (bf16[1,1,3584,256]{3,2,1,0:T(8,128)(2,1)S(1)}, bf16[1,1,3584,256]{3,2,1,0:T(8,128)(2,1)}, u32[]{:S(2)}) copy-start(bf16[1,1,3584,256]{3,2,1,0:T(8,128)(2,1)} %param.15) | copy-start | bytes 5505028
  110.2 15.3 %collective-permute-start.12 = (bf16[64,3584]{1,0:T(8,128)(2,1)S(1)}, bf16[64,3584]{1,0:T(8,128)(2,1)S(1)}, u32[]{:S(2)}, u32[]{:S(2)}) collective-permute-start(bf16[64,3584]{1,0:T(8,128)(2,1)S(1)} %slice.49), channel_id=1, source_target_pairs={{0,4},{1,5},{2,6},{3,7},{4,0},{5,1},{6,2},{7,3},{8,12},{9,13},{10,... | collective-permute-start | bytes 1376264 | tf_op jit(solution)/shard_map/ppermute | solution.py:39
  113.7 19.5 %collective-permute-start.11 = (bf16[64,3584]{1,0:T(8,128)(2,1)S(1)}, bf16[64,3584]{1,0:T(8,128)(2,1)S(1)}, u32[]{:S(2)}, u32[]{:S(2)}) collective-permute-start(bf16[64,3584]{1,0:T(8,128)(2,1)S(1)} %slice.47), channel_id=1, source_target_pairs={{0,4},{1,5},{2,6},{3,7},{4,0},{5,1},{6,2},{7,3},{8,12},{9,13},{10,... | collective-permute-start | bytes 1376264 | tf_op jit(solution)/shard_map/ppermute | solution.py:39
  133.3 52.6 %copy-start.5 = (bf16[64,3584]{1,0:T(8,128)(2,1)S(1)}, bf16[64,3584]{1,0:T(8,128)(2,1)}, u32[]{:S(2)}) copy-start(bf16[64,3584]{1,0:T(8,128)(2,1)} %copy-done.4) | copy-start | bytes 1376260

commit v4 on v3

--- a/solution.py
+++ b/solution.py
@@ -156,22 +156,16 @@
 
 
 def near_kernel(rows_fwd, rows_bwd, factor, *refs):
-    sources, part, grad_part, buffers, sems = refs[:6], refs[6], refs[7], refs[8:14], refs[14]
-    copies = fetch(sources, buffers, sems)
-    own_in, own_down, behind_in, behind, ahead_in, ahead = buffers
+    own_in, own_down, behind_in, behind, ahead_in, ahead, part, grad_part = refs
     count = rows_fwd.shape[1] // WIDTH
 
     def scaled(i, grad_act):
         rows = slice(i * 128, (i + 1) * 128)
         return slope(grad_act, factor[rows, :HIDDEN], factor[rows, HIDDEN:])
 
-    copies[0].wait()
-    copies[1].wait()
     acts = [activate(mm(rows_fwd[...], own_in[...]))]
     grads = [scaled(0, mt(rows_bwd[...], own_down[...]))]
     for i, near_in, near in ((1, behind_in, behind), (2, ahead_in, ahead)):
-        copies[2 * i].wait()
-        copies[2 * i + 1].wait()
         acts.append(activate(mm(rows_fwd[...], near_in[...])))
         grads.append(scaled(i, across_blocks(rows_bwd, near, 0)))
     for c in range(count):
@@ -317,8 +311,7 @@
     part, grad_part = call(
         near_kernel,
         [(narrow, jnp.float32)] * 2,
-        (rows_fwd, rows_bwd, factor),
-        (in_own, down_own, behind_in, behind, ahead_in, ahead),
+        (rows_fwd, rows_bwd, factor, in_own, down_own, behind_in, behind, ahead_in, ahead),
         flops=2_000_000_000,
         traffic=0,
     )

time: 188 us -> 188 us (level)
  no operation moved by 1% of the time
where the time goes in v4:
time: 188 us; the launch traced here: 187 us
  waiting for transfers between devices  60.3 us (32%)
  blocking collectives  51.8 us (28%)
  starting transfers between devices  47.7 us (25%)
  Pallas kernels  17.4 us (9%)
  local copies, waits for them, and re-layouts  5.12 us (3%)
  other arithmetic  3.6 us (2%)
    all_to_all x1, blocking collectives, exchange_z(): lax.all_to_all(block, 'expert', split_axis=0, concat_axis=0, axis_index_g...  51.8 us
    ppermute x8, starting transfers between devices, shift_y(): return lax.ppermute(block, 'expert', route)  23.4 us
    ppermute x3, waiting for transfers between devices, swap_z(): return lax.ppermute(block, 'expert', [(k, k ^ ROWS) for k in range(size)])  22.5 us
    ppermute x8, waiting for transfers between devices, shift_y(): return lax.ppermute(block, 'expert', route)  21.7 us
    all_to_all x1, waiting for transfers between devices, exchange_z(): lax.all_to_all(block, 'expert', split_axis=0, concat_axis=0, axis_index_g...  16.1 us
    all_to_all x1, starting transfers between devices, exchange_z(): lax.all_to_all(block, 'expert', split_axis=0, concat_axis=0, axis_index_g...  14.9 us
    pallas_call x6, Pallas kernels, call(): pl.pallas_call(kernel, out_shape=[jax.ShapeDtypeStruct(shape, dtype) for...  11.4 us
    ppermute x3, starting transfers between devices, swap_z(): return lax.ppermute(block, 'expert', [(k, k ^ ROWS) for k in range(size)])  7.75 us
  transfers between devices with their start and end apart: 14, of which 8 were waited for; matrix products, arithmetic and copies ran while one was open for 3% of the time, Pallas kernels for 8%

profile of v4, /device:TPU:90, one launch (start us, length us, event | category | flops | bytes accessed | tf_op | source)
XLA Modules:
  0.0 186.9 jit_solution(2519995267690328134)
XLA Ops:
  2.4 2.1 %collective-permute-start.2 = (bf16[3584,256]{1,0:T(8,128)(2,1)}, bf16[3584,256]{1,0:T(8,128)(2,1)S(1)}, u32[]{:S(2)}, u32[]{:S(2)}) collective-permute-start(bf16[3584,256]{1,0:T(8,128)(2,1)} %bitcast.51), channel_id=1, source_target_pairs={{0,1},{1,2},{2,3},{3,0},{4,5},{5,6},{6,7},{7,4},{8,9},{9,10},{10,1... | collective-permute-start | bytes 5505032 | tf_op jit(solution)/shard_map/ppermute | solution.py:34
  4.5 3.7 %collective-permute-start.3 = (bf16[3584,256]{1,0:T(8,128)(2,1)}, bf16[3584,256]{1,0:T(8,128)(2,1)}, u32[]{:S(2)}, u32[]{:S(2)}) collective-permute-start(bf16[3584,256]{1,0:T(8,128)(2,1)} %bitcast.52), channel_id=1, source_target_pairs={{0,3},{1,0},{2,1},{3,2},{4,7},{5,4},{6,5},{7,6},{8,11},{9,8},{10,9... | collective-permute-start | bytes 5505032 | tf_op jit(solution)/shard_map/ppermute | solution.py:34
  11.4 14.9 %all-to-all-start = ((bf16[8,16,3584]{2,1,0:T(8,128)(2,1)}), bf16[8,16,3584]{2,1,0:T(8,128)(2,1)}, u32[]{:S(2)}, u32[]{:S(2)}) async-start(bf16[8,16,3584]{2,1,0:T(8,128)(2,1)} %bitcast.4), calls=%async_computation | async-start | bytes 1835008 | tf_op jit(solution)/shard_map/all_to_all | solution.py:44
  27.6 3.3 %shard_map.124 = (bf16[2048,256]{1,0:T(8,128)(2,1)}, bf16[2048,256]{1,0:T(8,128)(2,1)}) custom-call(bf16[128,3584]{1,0:T(8,128)(2,1)} %bitcast.49, bf16[128,256]{1,0:T(8,128)(2,1)} %get-tuple-element.42.saved_across, bf16[128,256]{1,0:T(8,128)(2,1)} %get-tuple-element.43.saved_next, bf16[128,256]{1,0:T(8,128)(2,1)} %maximum_bitcast_fusion.2.saved_previous), custom_call_target="tpu_custom_call" | custom-call | bytes 2000000 | tf_op jit(solution)/shard_map/pallas_call | solution.py:258
  30.9 3.3 %collective-permute-start.7 = (bf16[2048,256]{1,0:T(8,128)(2,1)}, bf16[2048,256]{1,0:T(8,128)(2,1)S(1)}, u32[]{:S(2)}, u32[]{:S(2)}) collective-permute-start(bf16[2048,256]{1,0:T(8,128)(2,1)} %get-tuple-element.20), channel_id=1, source_target_pairs={{0,1},{1,2},{2,3},{3,0},{4,5},{5,6},{6,7},{7,4},{8,9},{9,10},{10,1... | collective-permute-start | bytes 3145736 | tf_op jit(solution)/shard_map/ppermute | solution.py:34
  34.2 2.5 %collective-permute-start.8 = (bf16[2048,256]{1,0:T(8,128)(2,1)}, bf16[2048,256]{1,0:T(8,128)(2,1)}, u32[]{:S(2)}, u32[]{:S(2)}) collective-permute-start(bf16[2048,256]{1,0:T(8,128)(2,1)} %get-tuple-element.23), channel_id=1, source_target_pairs={{0,3},{1,0},{2,1},{3,2},{4,7},{5,4},{6,5},{7,6},{8,11},{9,8},{10,9... | collective-permute-start | bytes 3145736 | tf_op jit(solution)/shard_map/ppermute | solution.py:34
  36.8 10.6 %collective-permute-done.2.behind.refs_2_ = bf16[3584,256]{1,0:T(8,128)(2,1)S(1)} collective-permute-done((bf16[3584,256]{1,0:T(8,128)(2,1)}, bf16[3584,256]{1,0:T(8,128)(2,1)S(1)}, u32[]{:S(2)}, u32[]{:S(2)}) %collective-permute-start.2) | collective-permute-done | bytes 1835040 | tf_op jit(solution)/shard_map/ppermute | solution.py:34
  47.4 3.5 %collective-permute-done.3.ahead.refs_4_ = bf16[3584,256]{1,0:T(8,128)(2,1)} collective-permute-done((bf16[3584,256]{1,0:T(8,128)(2,1)}, bf16[3584,256]{1,0:T(8,128)(2,1)}, u32[]{:S(2)}, u32[]{:S(2)}) %collective-permute-start.3) | collective-permute-done | bytes 1835040 | tf_op jit(solution)/shard_map/ppermute | solution.py:34
  50.9 2.7 %shard_map.123 = (bf16[1792,256]{1,0:T(8,128)(2,1)}, bf16[1792,256]{1,0:T(8,128)(2,1)}) custom-call(bf16[3584,256]{1,0:T(8,128)(2,1)} %copy-done.2, bf16[3584,256]{1,0:T(8,128)(2,1)} %collective-permute-done.3.ahead.refs_4_), custom_call_target="tpu_custom_call" | custom-call | flops 20000000000 | bytes 4000000 | tf_op jit(solution)/shard_map/pallas_call | solution.py:283
  53.6 2.3 %collective-permute-start.4 = (bf16[1792,256]{1,0:T(8,128)(2,1)}, bf16[1792,256]{1,0:T(8,128)(2,1)S(1)}, u32[]{:S(2)}, u32[]{:S(2)}) collective-permute-start(bf16[1792,256]{1,0:T(8,128)(2,1)} %get-tuple-element.18), channel_id=1, source_target_pairs={{0,1},{1,2},{2,3},{3,0},{4,5},{5,6},{6,7},{7,4},{8,9},{9,10},{10,1... | collective-permute-start | bytes 2752520 | tf_op jit(solution)/shard_map/ppermute | solution.py:34
  55.9 3.6 %collective-permute-start.5 = (bf16[1792,256]{1,0:T(8,128)(2,1)}, bf16[1792,256]{1,0:T(8,128)(2,1)S(1)}, u32[]{:S(2)}, u32[]{:S(2)}) collective-permute-start(bf16[1792,256]{1,0:T(8,128)(2,1)} %get-tuple-element.19), channel_id=1, source_target_pairs={{0,3},{1,0},{2,1},{3,2},{4,7},{5,4},{6,5},{7,6},{8,11},{9,8},{10,9... | collective-permute-start | bytes 2752520 | tf_op jit(solution)/shard_map/ppermute | solution.py:34
  59.5 16.1 %all-to-all-done = bf16[8,16,3584]{2,1,0:T(8,128)(2,1)} async-done(((bf16[8,16,3584]{2,1,0:T(8,128)(2,1)}), bf16[8,16,3584]{2,1,0:T(8,128)(2,1)}, u32[]{:S(2)}, u32[]{:S(2)}) %all-to-all-start) | async-done | bytes 917536 | tf_op jit(solution)/shard_map/all_to_all | solution.py:44
  75.5 1.9 %collective-permute-start.6 = (bf16[8,16,3584]{2,1,0:T(8,128)(2,1)}, bf16[8,16,3584]{2,1,0:T(8,128)(2,1)S(1)}, u32[]{:S(2)}, u32[]{:S(2)}) collective-permute-start(bf16[8,16,3584]{2,1,0:T(8,128)(2,1)} %all-to-all-done), channel_id=1, source_target_pairs={{0,4},{1,5},{2,6},{3,7},{4,0},{5,1},{6,2},{7,3},{8,12},{9,13},{10,... | collective-permute-start | bytes 2752520 | tf_op jit(solution)/shard_map/ppermute | solution.py:39
  77.5 2.1 %collective-permute-start.9 = (bf16[1024,256]{1,0:T(8,128)(2,1)S(1)}, bf16[1024,256]{1,0:T(8,128)(2,1)S(1)}, u32[]{:S(2)}, u32[]{:S(2)}) collective-permute-start(bf16[1024,256]{1,0:T(8,128)(2,1)S(1)} %slice.44), channel_id=1, source_target_pairs={{0,1},{1,2},{2,3},{3,0},{4,5},{5,6},{6,7},{7,4},{8,9},{9,10},{10,1... | collective-permute-start | bytes 1572872 | tf_op jit(solution)/shard_map/ppermute | solution.py:34
  80.7 3.7 %collective-permute-start.10 = (bf16[896,256]{1,0:T(8,128)(2,1)S(1)}, bf16[896,256]{1,0:T(8,128)(2,1)S(1)}, u32[]{:S(2)}, u32[]{:S(2)}) collective-permute-start(bf16[896,256]{1,0:T(8,128)(2,1)S(1)} %slice.45), channel_id=1, source_target_pairs={{0,3},{1,0},{2,1},{3,2},{4,7},{5,4},{6,5},{7,6},{8,11},{9,8},{10,9... | collective-permute-start | bytes 1376264 | tf_op jit(solution)/shard_map/ppermute | solution.py:34
  85.3 4.2 %collective-permute-done.4.refs_0_ = bf16[1792,256]{1,0:T(8,128)(2,1)S(1)} collective-permute-done((bf16[1792,256]{1,0:T(8,128)(2,1)}, bf16[1792,256]{1,0:T(8,128)(2,1)S(1)}, u32[]{:S(2)}, u32[]{:S(2)}) %collective-permute-start.4) | collective-permute-done | bytes 917536 | tf_op jit(solution)/shard_map/ppermute | solution.py:34
  89.5 3.4 %collective-permute-done.5.refs_1_ = bf16[1792,256]{1,0:T(8,128)(2,1)S(1)} collective-permute-done((bf16[1792,256]{1,0:T(8,128)(2,1)}, bf16[1792,256]{1,0:T(8,128)(2,1)S(1)}, u32[]{:S(2)}, u32[]{:S(2)}) %collective-permute-start.5) | collective-permute-done | bytes 917536 | tf_op jit(solution)/shard_map/ppermute | solution.py:34
  92.9 6.7 %collective-permute-done.6 = bf16[8,16,3584]{2,1,0:T(8,128)(2,1)S(1)} collective-permute-done((bf16[8,16,3584]{2,1,0:T(8,128)(2,1)}, bf16[8,16,3584]{2,1,0:T(8,128)(2,1)S(1)}, u32[]{:S(2)}, u32[]{:S(2)}) %collective-permute-start.6) | collective-permute-done | bytes 917536 | tf_op jit(solution)/shard_map/ppermute | solution.py:39
  103.3 5.8 %shard_map.126 = (f32[128,3584]{1,0:T(8,128)S(1)}, f32[128,3584]{1,0:T(8,128)S(1)}) custom-call(bf16[128,3584]{1,0:T(8,128)(2,1)S(1)} %get-tuple-element.30.rows_fwd.rows, bf16[128,3584]{1,0:T(8,128)(2,1)S(1)} %get-tuple-element.31.rows_bwd.rows, f32[384,256]{1,0:T(8,128)S(1)} %shard_map.125.factor, bf16[3584,256]{1,0:T(8,128)(2,1)S(1)} %bitcast.53, ...), custom_call_target="tpu_custom_call" | custom-call | flops 2000000000 | tf_op jit(solution)/shard_map/pallas_call | solution.py:219
  110.6 2.2 %collective-permute-start.12 = (bf16[64,3584]{1,0:T(8,128)(2,1)S(1)}, bf16[64,3584]{1,0:T(8,128)(2,1)S(1)}, u32[]{:S(2)}, u32[]{:S(2)}) collective-permute-start(bf16[64,3584]{1,0:T(8,128)(2,1)S(1)} %slice.49), channel_id=1, source_target_pairs={{0,4},{1,5},{2,6},{3,7},{4,0},{5,1},{6,2},{7,3},{8,12},{9,13},{10,... | collective-permute-start | bytes 1376264 | tf_op jit(solution)/shard_map/ppermute | solution.py:39
  114.1 3.6 %collective-permute-start.11 = (bf16[64,3584]{1,0:T(8,128)(2,1)S(1)}, bf16[64,3584]{1,0:T(8,128)(2,1)S(1)}, u32[]{:S(2)}, u32[]{:S(2)}) collective-permute-start(bf16[64,3584]{1,0:T(8,128)(2,1)S(1)} %slice.47), channel_id=1, source_target_pairs={{0,4},{1,5},{2,6},{3,7},{4,0},{5,1},{6,2},{7,3},{8,12},{9,13},{10,... | collective-permute-start | bytes 1376264 | tf_op jit(solution)/shard_map/ppermute | solution.py:39
  117.7 8.2 %collective-permute-done.12 = bf16[64,3584]{1,0:T(8,128)(2,1)S(1)} collective-permute-done((bf16[64,3584]{1,0:T(8,128)(2,1)S(1)}, bf16[64,3584]{1,0:T(8,128)(2,1)S(1)}, u32[]{:S(2)}, u32[]{:S(2)}) %collective-permute-start.12) | collective-permute-done | bytes 458784 | tf_op jit(solution)/shard_map/ppermute | solution.py:39
  126.1 7.5 %collective-permute-done.11 = bf16[64,3584]{1,0:T(8,128)(2,1)S(1)} collective-permute-done((bf16[64,3584]{1,0:T(8,128)(2,1)S(1)}, bf16[64,3584]{1,0:T(8,128)(2,1)S(1)}, u32[]{:S(2)}, u32[]{:S(2)}) %collective-permute-start.11) | collective-permute-done | bytes 458784 | tf_op jit(solution)/shard_map/ppermute | solution.py:39
  133.8 51.8 %all_to_all.10 = bf16[8,16,3584]{2,1,0:T(8,128)(2,1)S(1)} all-to-all(bf16[8,16,3584]{2,1,0:T(8,128)(2,1)S(1)} %pad_maximum_fusion.1), channel_id=1, replica_groups={{0,8,16,24,32,40,48,56},{1,9,17,25,33,41,49,57},{2,10,18,26,34,42,50,58..., dimensions={0} | all-to-all | bytes 1835008 | tf_op jit(solution)/shard_map/all_to_all | solution.py:44
  (44 shorter events, 16.2 us)
Async XLA Ops:
  0.6 9.1 %collective-permute-start = (bf16[64,3584]{1,0:T(8,128)(2,1)}, bf16[64,3584]{1,0:T(8,128)(2,1)S(1)}, u32[]{:S(2)}, u32[]{:S(2)}) collective-permute-start(bf16[64,3584]{1,0:T(8,128)(2,1)} %bitcast.57), channel_id=1, source_target_pairs={{448,0},{0,64},{64,128},{128,192},{192,256},{256,320},{320,384},{3... | collective-permute-start | bytes 1376264 | tf_op jit(solution)/shard_map/ppermute | solution.py:28
  0.7 9.1 %collective-permute-start.1 = (bf16[64,3584]{1,0:T(8,128)(2,1)}, bf16[64,3584]{1,0:T(8,128)(2,1)S(1)}, u32[]{:S(2)}, u32[]{:S(2)}) collective-permute-start(bf16[64,3584]{1,0:T(8,128)(2,1)} %bitcast.58), channel_id=1, source_target_pairs={{64,0},{128,64},{192,128},{256,192},{320,256},{384,320},{448,384},... | collective-permute-start | bytes 1376264 | tf_op jit(solution)/shard_map/ppermute | solution.py:28
  2.4 45.0 %collective-permute-start.2 = (bf16[3584,256]{1,0:T(8,128)(2,1)}, bf16[3584,256]{1,0:T(8,128)(2,1)S(1)}, u32[]{:S(2)}, u32[]{:S(2)}) collective-permute-start(bf16[3584,256]{1,0:T(8,128)(2,1)} %bitcast.51), channel_id=1, source_target_pairs={{0,1},{1,2},{2,3},{3,0},{4,5},{5,6},{6,7},{7,4},{8,9},{9,10},{10,1... | collective-permute-start | bytes 5505032 | tf_op jit(solution)/shard_map/ppermute | solution.py:34
  4.5 46.3 %collective-permute-start.3 = (bf16[3584,256]{1,0:T(8,128)(2,1)}, bf16[3584,256]{1,0:T(8,128)(2,1)}, u32[]{:S(2)}, u32[]{:S(2)}) collective-permute-start(bf16[3584,256]{1,0:T(8,128)(2,1)} %bitcast.52), channel_id=1, source_target_pairs={{0,3},{1,0},{2,1},{3,2},{4,7},{5,4},{6,5},{7,6},{8,11},{9,8},{10,9... | collective-permute-start | bytes 5505032 | tf_op jit(solution)/shard_map/ppermute | solution.py:34
  9.8 1.7 copy-start.4
  11.4 14.9 %copy-start.6 = (bf16[1,1,512,256]{3,2,1,0:T(8,128)(2,1)S(1)}, bf16[1,1,512,256]{3,2,1,0:T(8,128)(2,1)}, u32[]{:S(2)}) copy-start(bf16[1,1,512,256]{3,2,1,0:T(8,128)(2,1)} %param.17) | copy-start | bytes 786436
  11.4 64.1 %all-to-all-start = ((bf16[8,16,3584]{2,1,0:T(8,128)(2,1)}), bf16[8,16,3584]{2,1,0:T(8,128)(2,1)}, u32[]{:S(2)}, u32[]{:S(2)}) async-start(bf16[8,16,3584]{2,1,0:T(8,128)(2,1)} %bitcast.4), calls=%async_computation | async-start | bytes 1835008 | tf_op jit(solution)/shard_map/all_to_all | solution.py:44
  30.9 46.6 %collective-permute-start.7 = (bf16[2048,256]{1,0:T(8,128)(2,1)}, bf16[2048,256]{1,0:T(8,128)(2,1)S(1)}, u32[]{:S(2)}, u32[]{:S(2)}) collective-permute-start(bf16[2048,256]{1,0:T(8,128)(2,1)} %get-tuple-element.20), channel_id=1, source_target_pairs={{0,1},{1,2},{2,3},{3,0},{4,5},{5,6},{6,7},{7,4},{8,9},{9,10},{10,1... | collective-permute-start | bytes 3145736 | tf_op jit(solution)/shard_map/ppermute | solution.py:34
  34.2 45.4 %collective-permute-start.8 = (bf16[2048,256]{1,0:T(8,128)(2,1)}, bf16[2048,256]{1,0:T(8,128)(2,1)}, u32[]{:S(2)}, u32[]{:S(2)}) collective-permute-start(bf16[2048,256]{1,0:T(8,128)(2,1)} %get-tuple-element.23), channel_id=1, source_target_pairs={{0,3},{1,0},{2,1},{3,2},{4,7},{5,4},{6,5},{7,6},{8,11},{9,8},{10,9... | collective-permute-start | bytes 3145736 | tf_op jit(solution)/shard_map/ppermute | solution.py:34
  47.4 3.5 %copy-start.2 = (bf16[3584,256]{1,0:T(8,128)(2,1)}, bf16[3584,256]{1,0:T(8,128)(2,1)S(1)}, u32[]{:S(2)}) copy-start(bf16[3584,256]{1,0:T(8,128)(2,1)S(1)} %collective-permute-done.2.behind.refs_2_) | copy-start | bytes 5505028
  53.6 35.9 %collective-permute-start.4 = (bf16[1792,256]{1,0:T(8,128)(2,1)}, bf16[1792,256]{1,0:T(8,128)(2,1)S(1)}, u32[]{:S(2)}, u32[]{:S(2)}) collective-permute-start(bf16[1792,256]{1,0:T(8,128)(2,1)} %get-tuple-element.18), channel_id=1, source_target_pairs={{0,1},{1,2},{2,3},{3,0},{4,5},{5,6},{6,7},{7,4},{8,9},{9,10},{10,1... | collective-permute-start | bytes 2752520 | tf_op jit(solution)/shard_map/ppermute | solution.py:34
  55.9 37.0 %collective-permute-start.5 = (bf16[1792,256]{1,0:T(8,128)(2,1)}, bf16[1792,256]{1,0:T(8,128)(2,1)S(1)}, u32[]{:S(2)}, u32[]{:S(2)}) collective-permute-start(bf16[1792,256]{1,0:T(8,128)(2,1)} %get-tuple-element.19), channel_id=1, source_target_pairs={{0,3},{1,0},{2,1},{3,2},{4,7},{5,4},{6,5},{7,6},{8,11},{9,8},{10,9... | collective-permute-start | bytes 2752520 | tf_op jit(solution)/shard_map/ppermute | solution.py:34
  75.5 24.1 %collective-permute-start.6 = (bf16[8,16,3584]{2,1,0:T(8,128)(2,1)}, bf16[8,16,3584]{2,1,0:T(8,128)(2,1)S(1)}, u32[]{:S(2)}, u32[]{:S(2)}) collective-permute-start(bf16[8,16,3584]{2,1,0:T(8,128)(2,1)} %all-to-all-done), channel_id=1, source_target_pairs={{0,4},{1,5},{2,6},{3,7},{4,0},{5,1},{6,2},{7,3},{8,12},{9,13},{10,... | collective-permute-start | bytes 2752520 | tf_op jit(solution)/shard_map/ppermute | solution.py:39
  77.5 31.6 %collective-permute-start.9 = (bf16[1024,256]{1,0:T(8,128)(2,1)S(1)}, bf16[1024,256]{1,0:T(8,128)(2,1)S(1)}, u32[]{:S(2)}, u32[]{:S(2)}) collective-permute-start(bf16[1024,256]{1,0:T(8,128)(2,1)S(1)} %slice.44), channel_id=1, source_target_pairs={{0,1},{1,2},{2,3},{3,0},{4,5},{5,6},{6,7},{7,4},{8,9},{9,10},{10,1... | collective-permute-start | bytes 1572872 | tf_op jit(solution)/shard_map/ppermute | solution.py:34
  80.7 28.4 %collective-permute-start.10 = (bf16[896,256]{1,0:T(8,128)(2,1)S(1)}, bf16[896,256]{1,0:T(8,128)(2,1)S(1)}, u32[]{:S(2)}, u32[]{:S(2)}) collective-permute-start(bf16[896,256]{1,0:T(8,128)(2,1)S(1)} %slice.45), channel_id=1, source_target_pairs={{0,3},{1,0},{2,1},{3,2},{4,7},{5,4},{6,5},{7,6},{8,11},{9,8},{10,9... | collective-permute-start | bytes 1376264 | tf_op jit(solution)/shard_map/ppermute | solution.py:34
  101.0 1.5 copy-start.3
  101.1 1.6 copy-start
  101.1 2.2 %copy-start.1 = (bf16[1,1,3584,256]{3,2,1,0:T(8,128)(2,1)S(1)}, bf16[1,1,3584,256]{3,2,1,0:T(8,128)(2,1)}, u32[]{:S(2)}) copy-start(bf16[1,1,3584,256]{3,2,1,0:T(8,128)(2,1)} %param.15) | copy-start | bytes 5505028
  110.6 15.3 %collective-permute-start.12 = (bf16[64,3584]{1,0:T(8,128)(2,1)S(1)}, bf16[64,3584]{1,0:T(8,128)(2,1)S(1)}, u32[]{:S(2)}, u32[]{:S(2)}) collective-permute-start(bf16[64,3584]{1,0:T(8,128)(2,1)S(1)} %slice.49), channel_id=1, source_target_pairs={{0,4},{1,5},{2,6},{3,7},{4,0},{5,1},{6,2},{7,3},{8,12},{9,13},{10,... | collective-permute-start | bytes 1376264 | tf_op jit(solution)/shard_map/ppermute | solution.py:39
  114.1 19.5 %collective-permute-start.11 = (bf16[64,3584]{1,0:T(8,128)(2,1)S(1)}, bf16[64,3584]{1,0:T(8,128)(2,1)S(1)}, u32[]{:S(2)}, u32[]{:S(2)}) collective-permute-start(bf16[64,3584]{1,0:T(8,128)(2,1)S(1)} %slice.47), channel_id=1, source_target_pairs={{0,4},{1,5},{2,6},{3,7},{4,0},{5,1},{6,2},{7,3},{8,12},{9,13},{10,... | collective-permute-start | bytes 1376264 | tf_op jit(solution)/shard_map/ppermute | solution.py:39
  133.7 51.8 %copy-start.5 = (bf16[64,3584]{1,0:T(8,128)(2,1)S(1)}, bf16[64,3584]{1,0:T(8,128)(2,1)}, u32[]{:S(2)}) copy-start(bf16[64,3584]{1,0:T(8,128)(2,1)} %copy-done.4) | copy-start | bytes 1376260

commit v5 on v4

--- a/solution.py
+++ b/solution.py
@@ -168,11 +168,12 @@
     for i, near_in, near in ((1, behind_in, behind), (2, ahead_in, ahead)):
         acts.append(activate(mm(rows_fwd[...], near_in[...])))
         grads.append(scaled(i, across_blocks(rows_bwd, near, 0)))
+    both = jnp.concatenate(acts[1:], axis=1)
     for c in range(count):
         columns = slice(c * WIDTH, (c + 1) * WIDTH)
         block = slice(c * HIDDEN, (c + 1) * HIDDEN)
         total = mm(acts[0], own_down[:, columns])
-        part[:, columns] = total + mm(acts[1], behind[block]) + mm(acts[2], ahead[block])
+        part[:, columns] = total + mm(both, jnp.concatenate([behind[block], ahead[block]], axis=0))
     for start, size in CHUNKS:
         columns = slice(start, start + size)
         total = mt(grads[0], own_in[columns])

time: 188 us -> 188 us (level)
  no operation moved by 1% of the time
where the time goes in v5:
time: 188 us; the launch traced here: 187 us
  waiting for transfers between devices  60.3 us (32%)
  blocking collectives  52.1 us (28%)
  starting transfers between devices  47.7 us (25%)
  Pallas kernels  17.3 us (9%)
  local copies, waits for them, and re-layouts  5.12 us (3%)
  other arithmetic  3.6 us (2%)
    all_to_all x1, blocking collectives, exchange_z(): lax.all_to_all(block, 'expert', split_axis=0, concat_axis=0, axis_index_g...  52.1 us
    ppermute x8, starting transfers between devices, shift_y(): return lax.ppermute(block, 'expert', route)  23.4 us
    ppermute x3, waiting for transfers between devices, swap_z(): return lax.ppermute(block, 'expert', [(k, k ^ ROWS) for k in range(size)])  22.5 us
    ppermute x8, waiting for transfers between devices, shift_y(): return lax.ppermute(block, 'expert', route)  21.7 us
    all_to_all x1, waiting for transfers between devices, exchange_z(): lax.all_to_all(block, 'expert', split_axis=0, concat_axis=0, axis_index_g...  16.1 us
    all_to_all x1, starting transfers between devices, exchange_z(): lax.all_to_all(block, 'expert', split_axis=0, concat_axis=0, axis_index_g...  14.9 us
    pallas_call x6, Pallas kernels, call(): pl.pallas_call(kernel, out_shape=[jax.ShapeDtypeStruct(shape, dtype) for...  11.3 us
    ppermute x3, starting transfers between devices, swap_z(): return lax.ppermute(block, 'expert', [(k, k ^ ROWS) for k in range(size)])  7.75 us
  transfers between devices with their start and end apart: 14, of which 8 were waited for; matrix products, arithmetic and copies ran while one was open for 3% of the time, Pallas kernels for 8%

profile of v5, /device:TPU:90, one launch (start us, length us, event | category | flops | bytes accessed | tf_op | source)
XLA Modules:
  0.0 187.0 jit_solution(17726059486790544231)
XLA Ops:
  2.4 2.1 %collective-permute-start.2 = (bf16[3584,256]{1,0:T(8,128)(2,1)}, bf16[3584,256]{1,0:T(8,128)(2,1)S(1)}, u32[]{:S(2)}, u32[]{:S(2)}) collective-permute-start(bf16[3584,256]{1,0:T(8,128)(2,1)} %bitcast.51), channel_id=1, source_target_pairs={{0,1},{1,2},{2,3},{3,0},{4,5},{5,6},{6,7},{7,4},{8,9},{9,10},{10,1... | collective-permute-start | bytes 5505032 | tf_op jit(solution)/shard_map/ppermute | solution.py:34
  4.5 3.7 %collective-permute-start.3 = (bf16[3584,256]{1,0:T(8,128)(2,1)}, bf16[3584,256]{1,0:T(8,128)(2,1)}, u32[]{:S(2)}, u32[]{:S(2)}) collective-permute-start(bf16[3584,256]{1,0:T(8,128)(2,1)} %bitcast.52), channel_id=1, source_target_pairs={{0,3},{1,0},{2,1},{3,2},{4,7},{5,4},{6,5},{7,6},{8,11},{9,8},{10,9... | collective-permute-start | bytes 5505032 | tf_op jit(solution)/shard_map/ppermute | solution.py:34
  11.4 14.9 %all-to-all-start = ((bf16[8,16,3584]{2,1,0:T(8,128)(2,1)}), bf16[8,16,3584]{2,1,0:T(8,128)(2,1)}, u32[]{:S(2)}, u32[]{:S(2)}) async-start(bf16[8,16,3584]{2,1,0:T(8,128)(2,1)} %bitcast.4), calls=%async_computation | async-start | bytes 1835008 | tf_op jit(solution)/shard_map/all_to_all | solution.py:44
  27.6 3.3 %shard_map.124 = (bf16[2048,256]{1,0:T(8,128)(2,1)}, bf16[2048,256]{1,0:T(8,128)(2,1)}) custom-call(bf16[128,3584]{1,0:T(8,128)(2,1)} %bitcast.49, bf16[128,256]{1,0:T(8,128)(2,1)} %get-tuple-element.42.saved_across, bf16[128,256]{1,0:T(8,128)(2,1)} %get-tuple-element.43.saved_next, bf16[128,256]{1,0:T(8,128)(2,1)} %maximum_bitcast_fusion.2.saved_previous), custom_call_target="tpu_custom_call" | custom-call | bytes 2000000 | tf_op jit(solution)/shard_map/pallas_call | solution.py:259
  30.9 3.3 %collective-permute-start.7 = (bf16[2048,256]{1,0:T(8,128)(2,1)}, bf16[2048,256]{1,0:T(8,128)(2,1)S(1)}, u32[]{:S(2)}, u32[]{:S(2)}) collective-permute-start(bf16[2048,256]{1,0:T(8,128)(2,1)} %get-tuple-element.20), channel_id=1, source_target_pairs={{0,1},{1,2},{2,3},{3,0},{4,5},{5,6},{6,7},{7,4},{8,9},{9,10},{10,1... | collective-permute-start | bytes 3145736 | tf_op jit(solution)/shard_map/ppermute | solution.py:34
  34.2 2.5 %collective-permute-start.8 = (bf16[2048,256]{1,0:T(8,128)(2,1)}, bf16[2048,256]{1,0:T(8,128)(2,1)}, u32[]{:S(2)}, u32[]{:S(2)}) collective-permute-start(bf16[2048,256]{1,0:T(8,128)(2,1)} %get-tuple-element.23), channel_id=1, source_target_pairs={{0,3},{1,0},{2,1},{3,2},{4,7},{5,4},{6,5},{7,6},{8,11},{9,8},{10,9... | collective-permute-start | bytes 3145736 | tf_op jit(solution)/shard_map/ppermute | solution.py:34
  36.8 10.6 %collective-permute-done.2.behind.refs_2_ = bf16[3584,256]{1,0:T(8,128)(2,1)S(1)} collective-permute-done((bf16[3584,256]{1,0:T(8,128)(2,1)}, bf16[3584,256]{1,0:T(8,128)(2,1)S(1)}, u32[]{:S(2)}, u32[]{:S(2)}) %collective-permute-start.2) | collective-permute-done | bytes 1835040 | tf_op jit(solution)/shard_map/ppermute | solution.py:34
  47.4 3.5 %collective-permute-done.3.ahead.refs_4_ = bf16[3584,256]{1,0:T(8,128)(2,1)} collective-permute-done((bf16[3584,256]{1,0:T(8,128)(2,1)}, bf16[3584,256]{1,0:T(8,128)(2,1)}, u32[]{:S(2)}, u32[]{:S(2)}) %collective-permute-start.3) | collective-permute-done | bytes 1835040 | tf_op jit(solution)/shard_map/ppermute | solution.py:34
  50.9 2.7 %shard_map.123 = (bf16[1792,256]{1,0:T(8,128)(2,1)}, bf16[1792,256]{1,0:T(8,128)(2,1)}) custom-call(bf16[3584,256]{1,0:T(8,128)(2,1)} %copy-done.2, bf16[3584,256]{1,0:T(8,128)(2,1)} %collective-permute-done.3.ahead.refs_4_), custom_call_target="tpu_custom_call" | custom-call | flops 20000000000 | bytes 4000000 | tf_op jit(solution)/shard_map/pallas_call | solution.py:284
  53.6 2.3 %collective-permute-start.4 = (bf16[1792,256]{1,0:T(8,128)(2,1)}, bf16[1792,256]{1,0:T(8,128)(2,1)S(1)}, u32[]{:S(2)}, u32[]{:S(2)}) collective-permute-start(bf16[1792,256]{1,0:T(8,128)(2,1)} %get-tuple-element.18), channel_id=1, source_target_pairs={{0,1},{1,2},{2,3},{3,0},{4,5},{5,6},{6,7},{7,4},{8,9},{9,10},{10,1... | collective-permute-start | bytes 2752520 | tf_op jit(solution)/shard_map/ppermute | solution.py:34
  55.9 3.6 %collective-permute-start.5 = (bf16[1792,256]{1,0:T(8,128)(2,1)}, bf16[1792,256]{1,0:T(8,128)(2,1)S(1)}, u32[]{:S(2)}, u32[]{:S(2)}) collective-permute-start(bf16[1792,256]{1,0:T(8,128)(2,1)} %get-tuple-element.19), channel_id=1, source_target_pairs={{0,3},{1,0},{2,1},{3,2},{4,7},{5,4},{6,5},{7,6},{8,11},{9,8},{10,9... | collective-permute-start | bytes 2752520 | tf_op jit(solution)/shard_map/ppermute | solution.py:34
  59.5 16.1 %all-to-all-done = bf16[8,16,3584]{2,1,0:T(8,128)(2,1)} async-done(((bf16[8,16,3584]{2,1,0:T(8,128)(2,1)}), bf16[8,16,3584]{2,1,0:T(8,128)(2,1)}, u32[]{:S(2)}, u32[]{:S(2)}) %all-to-all-start) | async-done | bytes 917536 | tf_op jit(solution)/shard_map/all_to_all | solution.py:44
  75.5 1.9 %collective-permute-start.6 = (bf16[8,16,3584]{2,1,0:T(8,128)(2,1)}, bf16[8,16,3584]{2,1,0:T(8,128)(2,1)S(1)}, u32[]{:S(2)}, u32[]{:S(2)}) collective-permute-start(bf16[8,16,3584]{2,1,0:T(8,128)(2,1)} %all-to-all-done), channel_id=1, source_target_pairs={{0,4},{1,5},{2,6},{3,7},{4,0},{5,1},{6,2},{7,3},{8,12},{9,13},{10,... | collective-permute-start | bytes 2752520 | tf_op jit(solution)/shard_map/ppermute | solution.py:39
  77.5 2.1 %collective-permute-start.9 = (bf16[1024,256]{1,0:T(8,128)(2,1)S(1)}, bf16[1024,256]{1,0:T(8,128)(2,1)S(1)}, u32[]{:S(2)}, u32[]{:S(2)}) collective-permute-start(bf16[1024,256]{1,0:T(8,128)(2,1)S(1)} %slice.44), channel_id=1, source_target_pairs={{0,1},{1,2},{2,3},{3,0},{4,5},{5,6},{6,7},{7,4},{8,9},{9,10},{10,1... | collective-permute-start | bytes 1572872 | tf_op jit(solution)/shard_map/ppermute | solution.py:34
  80.7 3.7 %collective-permute-start.10 = (bf16[896,256]{1,0:T(8,128)(2,1)S(1)}, bf16[896,256]{1,0:T(8,128)(2,1)S(1)}, u32[]{:S(2)}, u32[]{:S(2)}) collective-permute-start(bf16[896,256]{1,0:T(8,128)(2,1)S(1)} %slice.45), channel_id=1, source_target_pairs={{0,3},{1,0},{2,1},{3,2},{4,7},{5,4},{6,5},{7,6},{8,11},{9,8},{10,9... | collective-permute-start | bytes 1376264 | tf_op jit(solution)/shard_map/ppermute | solution.py:34
  85.3 4.2 %collective-permute-done.4.refs_0_ = bf16[1792,256]{1,0:T(8,128)(2,1)S(1)} collective-permute-done((bf16[1792,256]{1,0:T(8,128)(2,1)}, bf16[1792,256]{1,0:T(8,128)(2,1)S(1)}, u32[]{:S(2)}, u32[]{:S(2)}) %collective-permute-start.4) | collective-permute-done | bytes 917536 | tf_op jit(solution)/shard_map/ppermute | solution.py:34
  89.5 3.4 %collective-permute-done.5.refs_1_ = bf16[1792,256]{1,0:T(8,128)(2,1)S(1)} collective-permute-done((bf16[1792,256]{1,0:T(8,128)(2,1)}, bf16[1792,256]{1,0:T(8,128)(2,1)S(1)}, u32[]{:S(2)}, u32[]{:S(2)}) %collective-permute-start.5) | collective-permute-done | bytes 917536 | tf_op jit(solution)/shard_map/ppermute | solution.py:34
  92.9 6.7 %collective-permute-done.6 = bf16[8,16,3584]{2,1,0:T(8,128)(2,1)S(1)} collective-permute-done((bf16[8,16,3584]{2,1,0:T(8,128)(2,1)}, bf16[8,16,3584]{2,1,0:T(8,128)(2,1)S(1)}, u32[]{:S(2)}, u32[]{:S(2)}) %collective-permute-start.6) | collective-permute-done | bytes 917536 | tf_op jit(solution)/shard_map/ppermute | solution.py:39
  103.3 5.6 %shard_map.126 = (f32[128,3584]{1,0:T(8,128)S(1)}, f32[128,3584]{1,0:T(8,128)S(1)}) custom-call(bf16[128,3584]{1,0:T(8,128)(2,1)S(1)} %get-tuple-element.30.rows_fwd.rows, bf16[128,3584]{1,0:T(8,128)(2,1)S(1)} %get-tuple-element.31.rows_bwd.rows, f32[384,256]{1,0:T(8,128)S(1)} %shard_map.125.factor, bf16[3584,256]{1,0:T(8,128)(2,1)S(1)} %bitcast.53, ...), custom_call_target="tpu_custom_call" | custom-call | flops 2000000000 | tf_op jit(solution)/shard_map/pallas_call | solution.py:220
  110.5 2.2 %collective-permute-start.12 = (bf16[64,3584]{1,0:T(8,128)(2,1)S(1)}, bf16[64,3584]{1,0:T(8,128)(2,1)S(1)}, u32[]{:S(2)}, u32[]{:S(2)}) collective-permute-start(bf16[64,3584]{1,0:T(8,128)(2,1)S(1)} %slice.49), channel_id=1, source_target_pairs={{0,4},{1,5},{2,6},{3,7},{4,0},{5,1},{6,2},{7,3},{8,12},{9,13},{10,... | collective-permute-start | bytes 1376264 | tf_op jit(solution)/shard_map/ppermute | solution.py:39
  113.9 3.6 %collective-permute-start.11 = (bf16[64,3584]{1,0:T(8,128)(2,1)S(1)}, bf16[64,3584]{1,0:T(8,128)(2,1)S(1)}, u32[]{:S(2)}, u32[]{:S(2)}) collective-permute-start(bf16[64,3584]{1,0:T(8,128)(2,1)S(1)} %slice.47), channel_id=1, source_target_pairs={{0,4},{1,5},{2,6},{3,7},{4,0},{5,1},{6,2},{7,3},{8,12},{9,13},{10,... | collective-permute-start | bytes 1376264 | tf_op jit(solution)/shard_map/ppermute | solution.py:39
  117.6 8.2 %collective-permute-done.12 = bf16[64,3584]{1,0:T(8,128)(2,1)S(1)} collective-permute-done((bf16[64,3584]{1,0:T(8,128)(2,1)S(1)}, bf16[64,3584]{1,0:T(8,128)(2,1)S(1)}, u32[]{:S(2)}, u32[]{:S(2)}) %collective-permute-start.12) | collective-permute-done | bytes 458784 | tf_op jit(solution)/shard_map/ppermute | solution.py:39
  125.9 7.5 %collective-permute-done.11 = bf16[64,3584]{1,0:T(8,128)(2,1)S(1)} collective-permute-done((bf16[64,3584]{1,0:T(8,128)(2,1)S(1)}, bf16[64,3584]{1,0:T(8,128)(2,1)S(1)}, u32[]{:S(2)}, u32[]{:S(2)}) %collective-permute-start.11) | collective-permute-done | bytes 458784 | tf_op jit(solution)/shard_map/ppermute | solution.py:39
  133.6 52.1 %all_to_all.10 = bf16[8,16,3584]{2,1,0:T(8,128)(2,1)S(1)} all-to-all(bf16[8,16,3584]{2,1,0:T(8,128)(2,1)S(1)} %pad_maximum_fusion.1), channel_id=1, replica_groups={{0,8,16,24,32,40,48,56},{1,9,17,25,33,41,49,57},{2,10,18,26,34,42,50,58..., dimensions={0} | all-to-all | bytes 1835008 | tf_op jit(solution)/shard_map/all_to_all | solution.py:44
  (44 shorter events, 16.2 us)
Async XLA Ops:
  0.6 9.1 %collective-permute-start = (bf16[64,3584]{1,0:T(8,128)(2,1)}, bf16[64,3584]{1,0:T(8,128)(2,1)S(1)}, u32[]{:S(2)}, u32[]{:S(2)}) collective-permute-start(bf16[64,3584]{1,0:T(8,128)(2,1)} %bitcast.57), channel_id=1, source_target_pairs={{448,0},{0,64},{64,128},{128,192},{192,256},{256,320},{320,384},{3... | collective-permute-start | bytes 1376264 | tf_op jit(solution)/shard_map/ppermute | solution.py:28
  0.7 9.1 %collective-permute-start.1 = (bf16[64,3584]{1,0:T(8,128)(2,1)}, bf16[64,3584]{1,0:T(8,128)(2,1)S(1)}, u32[]{:S(2)}, u32[]{:S(2)}) collective-permute-start(bf16[64,3584]{1,0:T(8,128)(2,1)} %bitcast.58), channel_id=1, source_target_pairs={{64,0},{128,64},{192,128},{256,192},{320,256},{384,320},{448,384},... | collective-permute-start | bytes 1376264 | tf_op jit(solution)/shard_map/ppermute | solution.py:28
  2.4 45.0 %collective-permute-start.2 = (bf16[3584,256]{1,0:T(8,128)(2,1)}, bf16[3584,256]{1,0:T(8,128)(2,1)S(1)}, u32[]{:S(2)}, u32[]{:S(2)}) collective-permute-start(bf16[3584,256]{1,0:T(8,128)(2,1)} %bitcast.51), channel_id=1, source_target_pairs={{0,1},{1,2},{2,3},{3,0},{4,5},{5,6},{6,7},{7,4},{8,9},{9,10},{10,1... | collective-permute-start | bytes 5505032 | tf_op jit(solution)/shard_map/ppermute | solution.py:34
  4.5 46.3 %collective-permute-start.3 = (bf16[3584,256]{1,0:T(8,128)(2,1)}, bf16[3584,256]{1,0:T(8,128)(2,1)}, u32[]{:S(2)}, u32[]{:S(2)}) collective-permute-start(bf16[3584,256]{1,0:T(8,128)(2,1)} %bitcast.52), channel_id=1, source_target_pairs={{0,3},{1,0},{2,1},{3,2},{4,7},{5,4},{6,5},{7,6},{8,11},{9,8},{10,9... | collective-permute-start | bytes 5505032 | tf_op jit(solution)/shard_map/ppermute | solution.py:34
  9.8 1.7 copy-start.4
  11.4 14.9 %copy-start.6 = (bf16[1,1,512,256]{3,2,1,0:T(8,128)(2,1)S(1)}, bf16[1,1,512,256]{3,2,1,0:T(8,128)(2,1)}, u32[]{:S(2)}) copy-start(bf16[1,1,512,256]{3,2,1,0:T(8,128)(2,1)} %param.17) | copy-start | bytes 786436
  11.4 64.1 %all-to-all-start = ((bf16[8,16,3584]{2,1,0:T(8,128)(2,1)}), bf16[8,16,3584]{2,1,0:T(8,128)(2,1)}, u32[]{:S(2)}, u32[]{:S(2)}) async-start(bf16[8,16,3584]{2,1,0:T(8,128)(2,1)} %bitcast.4), calls=%async_computation | async-start | bytes 1835008 | tf_op jit(solution)/shard_map/all_to_all | solution.py:44
  30.9 46.6 %collective-permute-start.7 = (bf16[2048,256]{1,0:T(8,128)(2,1)}, bf16[2048,256]{1,0:T(8,128)(2,1)S(1)}, u32[]{:S(2)}, u32[]{:S(2)}) collective-permute-start(bf16[2048,256]{1,0:T(8,128)(2,1)} %get-tuple-element.20), channel_id=1, source_target_pairs={{0,1},{1,2},{2,3},{3,0},{4,5},{5,6},{6,7},{7,4},{8,9},{9,10},{10,1... | collective-permute-start | bytes 3145736 | tf_op jit(solution)/shard_map/ppermute | solution.py:34
  34.2 45.4 %collective-permute-start.8 = (bf16[2048,256]{1,0:T(8,128)(2,1)}, bf16[2048,256]{1,0:T(8,128)(2,1)}, u32[]{:S(2)}, u32[]{:S(2)}) collective-permute-start(bf16[2048,256]{1,0:T(8,128)(2,1)} %get-tuple-element.23), channel_id=1, source_target_pairs={{0,3},{1,0},{2,1},{3,2},{4,7},{5,4},{6,5},{7,6},{8,11},{9,8},{10,9... | collective-permute-start | bytes 3145736 | tf_op jit(solution)/shard_map/ppermute | solution.py:34
  47.4 3.5 %copy-start.2 = (bf16[3584,256]{1,0:T(8,128)(2,1)}, bf16[3584,256]{1,0:T(8,128)(2,1)S(1)}, u32[]{:S(2)}) copy-start(bf16[3584,256]{1,0:T(8,128)(2,1)S(1)} %collective-permute-done.2.behind.refs_2_) | copy-start | bytes 5505028
  53.6 35.9 %collective-permute-start.4 = (bf16[1792,256]{1,0:T(8,128)(2,1)}, bf16[1792,256]{1,0:T(8,128)(2,1)S(1)}, u32[]{:S(2)}, u32[]{:S(2)}) collective-permute-start(bf16[1792,256]{1,0:T(8,128)(2,1)} %get-tuple-element.18), channel_id=1, source_target_pairs={{0,1},{1,2},{2,3},{3,0},{4,5},{5,6},{6,7},{7,4},{8,9},{9,10},{10,1... | collective-permute-start | bytes 2752520 | tf_op jit(solution)/shard_map/ppermute | solution.py:34
  55.9 37.0 %collective-permute-start.5 = (bf16[1792,256]{1,0:T(8,128)(2,1)}, bf16[1792,256]{1,0:T(8,128)(2,1)S(1)}, u32[]{:S(2)}, u32[]{:S(2)}) collective-permute-start(bf16[1792,256]{1,0:T(8,128)(2,1)} %get-tuple-element.19), channel_id=1, source_target_pairs={{0,3},{1,0},{2,1},{3,2},{4,7},{5,4},{6,5},{7,6},{8,11},{9,8},{10,9... | collective-permute-start | bytes 2752520 | tf_op jit(solution)/shard_map/ppermute | solution.py:34
  75.5 24.1 %collective-permute-start.6 = (bf16[8,16,3584]{2,1,0:T(8,128)(2,1)}, bf16[8,16,3584]{2,1,0:T(8,128)(2,1)S(1)}, u32[]{:S(2)}, u32[]{:S(2)}) collective-permute-start(bf16[8,16,3584]{2,1,0:T(8,128)(2,1)} %all-to-all-done), channel_id=1, source_target_pairs={{0,4},{1,5},{2,6},{3,7},{4,0},{5,1},{6,2},{7,3},{8,12},{9,13},{10,... | collective-permute-start | bytes 2752520 | tf_op jit(solution)/shard_map/ppermute | solution.py:39
  77.5 31.4 %collective-permute-start.9 = (bf16[1024,256]{1,0:T(8,128)(2,1)S(1)}, bf16[1024,256]{1,0:T(8,128)(2,1)S(1)}, u32[]{:S(2)}, u32[]{:S(2)}) collective-permute-start(bf16[1024,256]{1,0:T(8,128)(2,1)S(1)} %slice.44), channel_id=1, source_target_pairs={{0,1},{1,2},{2,3},{3,0},{4,5},{5,6},{6,7},{7,4},{8,9},{9,10},{10,1... | collective-permute-start | bytes 1572872 | tf_op jit(solution)/shard_map/ppermute | solution.py:34
  80.7 28.3 %collective-permute-start.10 = (bf16[896,256]{1,0:T(8,128)(2,1)S(1)}, bf16[896,256]{1,0:T(8,128)(2,1)S(1)}, u32[]{:S(2)}, u32[]{:S(2)}) collective-permute-start(bf16[896,256]{1,0:T(8,128)(2,1)S(1)} %slice.45), channel_id=1, source_target_pairs={{0,3},{1,0},{2,1},{3,2},{4,7},{5,4},{6,5},{7,6},{8,11},{9,8},{10,9... | collective-permute-start | bytes 1376264 | tf_op jit(solution)/shard_map/ppermute | solution.py:34
  101.0 1.5 copy-start.3
  101.1 1.6 copy-start
  101.1 2.2 %copy-start.1 = (bf16[1,1,3584,256]{3,2,1,0:T(8,128)(2,1)S(1)}, bf16[1,1,3584,256]{3,2,1,0:T(8,128)(2,1)}, u32[]{:S(2)}) copy-start(bf16[1,1,3584,256]{3,2,1,0:T(8,128)(2,1)} %param.15) | copy-start | bytes 5505028
  110.5 15.3 %collective-permute-start.12 = (bf16[64,3584]{1,0:T(8,128)(2,1)S(1)}, bf16[64,3584]{1,0:T(8,128)(2,1)S(1)}, u32[]{:S(2)}, u32[]{:S(2)}) collective-permute-start(bf16[64,3584]{1,0:T(8,128)(2,1)S(1)} %slice.49), channel_id=1, source_target_pairs={{0,4},{1,5},{2,6},{3,7},{4,0},{5,1},{6,2},{7,3},{8,12},{9,13},{10,... | collective-permute-start | bytes 1376264 | tf_op jit(solution)/shard_map/ppermute | solution.py:39
  113.9 19.5 %collective-permute-start.11 = (bf16[64,3584]{1,0:T(8,128)(2,1)S(1)}, bf16[64,3584]{1,0:T(8,128)(2,1)S(1)}, u32[]{:S(2)}, u32[]{:S(2)}) collective-permute-start(bf16[64,3584]{1,0:T(8,128)(2,1)S(1)} %slice.47), channel_id=1, source_target_pairs={{0,4},{1,5},{2,6},{3,7},{4,0},{5,1},{6,2},{7,3},{8,12},{9,13},{10,... | collective-permute-start | bytes 1376264 | tf_op jit(solution)/shard_map/ppermute | solution.py:39
  133.6 52.2 %copy-start.5 = (bf16[64,3584]{1,0:T(8,128)(2,1)S(1)}, bf16[64,3584]{1,0:T(8,128)(2,1)}, u32[]{:S(2)}) copy-start(bf16[64,3584]{1,0:T(8,128)(2,1)} %copy-done.4) | copy-start | bytes 1376260
